TPU v7x, 512 devices: a whole 4x4x16 slice. The times are simulated.
512 devices in a mesh: rep: 32 (over y_lo, z), fsdp: 16 (over x, y_hi, core).
Axes of the slice: x: 4, y: 4 (y_hi: 2, y_lo: 2; y = y_hi * 2 + y_lo), z: 16, core: 2. Of those that a mesh axis runs over, the one named last changes fastest.
Arguments:
- acts: bfloat16 [98304, 4096], P(('rep', 'fsdp')), may hold values from -24 to 24
- grad_out: bfloat16 [98304, 512], P(('rep', 'fsdp')), may hold values from -0.25 to 0.25
- inner_weight: bfloat16 [32, 4096, 512], P('rep', 'fsdp'), may hold values from -6 to 6
- adam_first: bfloat16 [32, 4096, 512], P('rep', 'fsdp'), may hold values from -6 to 6
- adam_second: bfloat16 [32, 4096, 512], P('rep', 'fsdp'), may hold values from 0.5 to 8
- global_weight: float32 [16, 32, 8, 512], P('fsdp', 'rep'), may hold values from -6 to 6
- outer_momentum: float32 [16, 32, 8, 512], P('fsdp', 'rep'), may hold values from -4 to 4
Outputs:
- input_grad: bfloat16 [98304, 4096], P(('rep', 'fsdp'))
- new_weight: bfloat16 [32, 4096, 512], P('rep', 'fsdp')
- new_first: bfloat16 [32, 4096, 512], P('rep', 'fsdp')
- new_second: bfloat16 [32, 4096, 512], P('rep', 'fsdp')
- new_global: float32 [16, 32, 8, 512], P('fsdp', 'rep')
- new_momentum: float32 [16, 32, 8, 512], P('fsdp', 'rep')
All inputs are finite; a program needn't handle non-finite values.
Results may differ from a plain program's by a relative error of at most 0.015.
Values may be sent and summed in bfloat16 or wider, within the bound.
No kernel may reach another device: no remote copies, remote signals or barrier semaphores. Data moves between devices by JAX's collectives and lax.ppermute only.
A program may use at most 64 MiB of HBM per device.

v0:
```python
import jax
import jax.numpy as jnp
from jax import lax
from jax.sharding import PartitionSpec as P

STEP = 10


momentum_coef = 0.9
outer_rate = 0.7
beta_first = 0.9
beta_second = 0.95
inner_rate = 0.25
decay_rate = 0.1
epsilon_adam = 1e-08
mix_factor = 0.5


def shards(acts, grad_out, inner_weight, adam_first, adam_second, global_weight, outer_momentum):
    weight = inner_weight[0]
    input_grad = jnp.einsum(
        "tk,ik->ti",
        grad_out,
        lax.all_gather(inner_weight, "fsdp", axis=1, tiled=True)[0],
        preferred_element_type=jnp.float32,
    ).astype(jnp.bfloat16)
    grads = lax.psum_scatter(
        jnp.einsum("ti,tk->ik", acts, grad_out, preferred_element_type=jnp.float32).astype(
            jnp.bfloat16
        ),
        "fsdp",
        scatter_dimension=0,
        tiled=True,
    ).astype(jnp.float32)
    slice_rows = global_weight.shape[2]
    global_slice = global_weight[0, 0]
    momentum = outer_momentum[0, 0]
    weight_wide = weight.astype(jnp.float32)
    total = lax.psum(weight_wide.astype(jnp.bfloat16), "rep").astype(jnp.float32)
    own_slice = lax.dynamic_slice_in_dim(total, lax.axis_index("rep") * slice_rows, slice_rows, 0)
    replica_mean = own_slice / lax.axis_size("rep")
    outer_delta = global_slice - replica_mean
    momentum_new = momentum_coef * momentum + outer_delta
    global_new = global_slice - outer_rate * (outer_delta + momentum_coef * momentum_new)
    global_rows = lax.all_gather(global_new, "rep", axis=0, tiled=True)
    first = beta_first * adam_first[0].astype(jnp.float32) + (1.0 - beta_first) * grads
    second = beta_second * adam_second[0].astype(jnp.float32) + (1.0 - beta_second) * grads * grads
    first_hat = first / (1.0 - beta_first**STEP)
    second_hat = second / (1.0 - beta_second**STEP)
    adamw = weight_wide - inner_rate * (
        first_hat / (jnp.sqrt(second_hat) + epsilon_adam) + decay_rate * weight_wide
    )
    new_weight = (mix_factor * adamw + (1.0 - mix_factor) * global_rows).astype(jnp.bfloat16)
    return (
        input_grad,
        new_weight[None],
        first.astype(jnp.bfloat16)[None],
        second.astype(jnp.bfloat16)[None],
        global_new[None, None],
        momentum_new[None, None],
    )


def solution(mesh):
    return jax.shard_map(
        shards,
        mesh=mesh,
        in_specs=(
            P(("rep", "fsdp"), None),
            P(("rep", "fsdp"), None),
            P("rep", "fsdp", None),
            P("rep", "fsdp", None),
            P("rep", "fsdp", None),
            P("fsdp", "rep", None, None),
            P("fsdp", "rep", None, None),
        ),
        out_specs=(
            P(("rep", "fsdp"), None),
            P("rep", "fsdp", None),
            P("rep", "fsdp", None),
            P("rep", "fsdp", None),
            P("fsdp", "rep", None, None),
            P("fsdp", "rep", None, None),
        ),
        check_vma=False,
    )
```

profile of v0, /device:TPU:2, one launch (start us, length us, event | category | flops | bytes accessed | tf_op | source)
XLA Modules:
  0.0 351.1 jit_solution(12033720167594658448)
XLA Ops:
  8.0 0.0 copy-start
  8.0 0.0 all-reduce.2.cloned.1.call-start
  8.1 0.7 all-reduce.2.cloned.1.call-update
  8.7 0.0 reduce-scatter.2.cloned.1.call-start
  8.8 0.6 copy-done
  9.4 4.2 %convolution_convert_fusion = bf16[4096,512]{1,0:T(8,128)(2,1)} fusion(bf16[192,4096]{1,0:T(8,128)(2,1)S(1)} %copy-done, bf16[192,512]{1,0:T(8,128)(2,1)} %param.8), kind=kOutput, calls=%fused_computation | convolution fusion | flops 807403520 | bytes 5963776 | tf_op jit(solution)/shard_map/ti,tk->ik/dot_general | solution.py:28
  13.6 0.0 copy-start.6
  13.6 0.0 copy-start.7
  13.6 0.0 copy-start.1
  13.6 0.0 copy-start.3
  13.6 0.0 copy-start.4
  13.6 0.0 copy-start.2
  13.6 0.0 reduce-scatter.2.cloned.1.call-update
  13.7 0.0 all-gather.2.cloned.1.call-start
  13.7 0.5 all-gather.2.cloned.1.call-update
  14.3 256.6 %all-reduce.2.cloned.1.call-done = bf16[256,512]{1,0:T(8,128)(2,1)} async-done(((bf16[256,512]{1,0:T(8,128)(2,1)}), bf16[256,512]{1,0:T(8,128)(2,1)}) %all-reduce.2.cloned.1.call-update) | async-done | bytes 262160 | tf_op jit(solution)/shard_map/psum | solution.py:39
  270.9 0.0 copy-done.6
  270.9 0.0 copy-done.7
  270.9 1.3 fusion.13
  272.2 0.0 copy-start.5
  272.2 64.1 %all_gather.7 = f32[256,512]{1,0:T(8,128)S(1)} all-gather(f32[8,512]{1,0:T(8,128)S(1)} %get-tuple-element.10), channel_id=1, replica_groups=mesh['rep'=32,'fsdp'=16] {'rep'}, dimensions={0}, use_global_device_ids=true | all-gather | bytes 540672 | tf_op jit(solution)/shard_map/all_gather | solution.py:45
  336.3 0.0 reduce-scatter.2.cloned.1.call-done
  336.3 0.0 copy-done.1
  336.3 0.0 copy-done.3
  336.3 0.0 copy-done.4
  336.3 2.5 fusion.10
  338.8 0.0 all-gather.2.cloned.1.call-done
  338.8 0.0 copy-done.2
  338.8 4.8 %convolution_convert_fusion.1 = bf16[192,4096]{1,0:T(8,128)(2,1)} fusion(bf16[192,512]{1,0:T(8,128)(2,1)S(1)} %copy-done.2, bf16[1,4096,512]{2,1,0:T(8,128)(2,1)} %all-gather.2.cloned.1.call-done), kind=kOutput, calls=%fused_computation.1 | convolution fusion | flops 806092800 | bytes 5963776 | tf_op jit(solution)/shard_map/tk,ik->ti/dot_general | solution.py:21
  343.6 0.0 copy-done.5
Async XLA Ops:
  8.0 1.4 copy-start
  8.0 262.9 %all-reduce.2.cloned.1.call-start = ((), (), s32[]{:S(2)}) async-start(), calls=%async_computation.3 | async-start | bytes 524288 | tf_op jit(solution)/shard_map/psum | solution.py:39
  8.7 327.5 %reduce-scatter.2.cloned.1.call-start = ((), (), s32[]{:S(2)}) async-start(), calls=%async_computation.2 | async-start | bytes 4456448 | tf_op jit(solution)/shard_map/reduce_scatter | solution.py:27
  13.6 257.3 %copy-start.6 = (f32[1,1,8,512]{3,2,1,0:T(8,128)S(1)}, f32[1,1,8,512]{3,2,1,0:T(8,128)}, u32[]{:S(2)}) copy-start(f32[1,1,8,512]{3,2,1,0:T(8,128)} %param.12) | copy-start | bytes 49156
  13.6 257.3 %copy-start.7 = (f32[1,1,8,512]{3,2,1,0:T(8,128)S(1)}, f32[1,1,8,512]{3,2,1,0:T(8,128)}, u32[]{:S(2)}) copy-start(f32[1,1,8,512]{3,2,1,0:T(8,128)} %param.13) | copy-start | bytes 49156
  13.6 322.7 %copy-start.1 = (bf16[1,256,512]{2,1,0:T(8,128)(2,1)S(1)}, bf16[1,256,512]{2,1,0:T(8,128)(2,1)}, u32[]{:S(2)}) copy-start(bf16[1,256,512]{2,1,0:T(8,128)(2,1)} %param.9) | copy-start | bytes 786436
  13.6 322.7 %copy-start.3 = (bf16[1,256,512]{2,1,0:T(8,128)(2,1)S(1)}, bf16[1,256,512]{2,1,0:T(8,128)(2,1)}, u32[]{:S(2)}) copy-start(bf16[1,256,512]{2,1,0:T(8,128)(2,1)} %param.11) | copy-start | bytes 786436
  13.6 322.7 %copy-start.4 = (bf16[1,256,512]{2,1,0:T(8,128)(2,1)S(1)}, bf16[1,256,512]{2,1,0:T(8,128)(2,1)}, u32[]{:S(2)}) copy-start(bf16[1,256,512]{2,1,0:T(8,128)(2,1)} %param.10) | copy-start | bytes 786436
  13.6 325.2 %copy-start.2 = (bf16[192,512]{1,0:T(8,128)(2,1)S(1)}, bf16[192,512]{1,0:T(8,128)(2,1)}, u32[]{:S(2)}) copy-start(bf16[192,512]{1,0:T(8,128)(2,1)} %param.8) | copy-start | bytes 589828
  13.7 325.1 %all-gather.2.cloned.1.call-start = ((), (), s32[]{:S(2)}) async-start(), calls=%async_computation.1 | async-start | bytes 4456448 | tf_op jit(solution)/shard_map/all_gather | solution.py:24
  272.2 71.4 %copy-start.5 = (f32[8,512]{1,0:T(8,128)}, f32[8,512]{1,0:T(8,128)S(1)}, u32[]{:S(2)}) copy-start(f32[8,512]{1,0:T(8,128)S(1)} %get-tuple-element.10) | copy-start | bytes 49156
Sparse Core Ops, SparseCore 0:
  12.0 258.8 all-reduce.1
Sparse Core Ops, SparseCore 1:
  14.1 107.6 reduce-scatter.1
  125.5 70.9 all-gather.1
where the time goes:
time: 351 us
  waiting for transfers between devices  258 us (74%)
  blocking collectives  64.1 us (18%)
  between operations  15.5 us (4%)
  matrix products  9.04 us (3%)
  other arithmetic  3.81 us (1%)
    psum x1, waiting for transfers between devices, shards(): lax.psum(weight_wide.astype(jnp.bfloat16), 'rep').astype(jnp.float32)  257 us
    all_gather x1, blocking collectives, shards(): global_rows = lax.all_gather(global_new, 'rep', axis=0, tiled=True)  64.1 us
  transfers between devices with their start and end apart: 3, of which 1 were waited for; matrix products, arithmetic and copies ran while one was open for 2% of the time, Pallas kernels for 0%

commit v1 on v0

v1 whole, which is shorter than its diff:
```python
import functools

import jax
import jax.numpy as jnp
from jax import lax
from jax.experimental import pallas as pl
from jax.experimental.pallas import tpu as pltpu
from jax.sharding import Mesh, PartitionSpec as P

STEP = 10

momentum_coef = 0.9
outer_rate = 0.7
beta_first = 0.9
beta_second = 0.95
inner_rate = 0.25
decay_rate = 0.1
epsilon_adam = 1e-08
mix_factor = 0.5

AXES = ("ylo", "zhi", "zlo", "x", "yhi", "core")
SIZES = (2, 4, 4, 4, 2, 2)
REP = ("ylo", "zhi", "zlo")
FSDP = ("x", "yhi", "core")
BF = jnp.bfloat16
F32 = jnp.float32


def permute(array, axis, size, shift):
    return lax.ppermute(array, axis, [(i, (i + shift) % size) for i in range(size)])


SCALE = outer_rate * (1.0 + momentum_coef) / 32


def share_of(globe, momentum):
    return (1.0 - outer_rate * (1.0 + momentum_coef)) * globe - (
        outer_rate * momentum_coef * momentum_coef
    ) * momentum


def call(kernel, operands, out_shape, name, loose=0, scratch=(), space=pl.ANY, weight=0, limit=40):
    fixed = len(operands) - loose
    return pl.pallas_call(
        kernel,
        in_specs=[pl.BlockSpec(memory_space=pltpu.VMEM)] * fixed
        + [pl.BlockSpec(memory_space=space)] * loose,
        out_shape=out_shape,
        scratch_shapes=scratch,
        compiler_params=pltpu.CompilerParams(vmem_limit_bytes=limit * 2**20),
        cost_estimate=pl.CostEstimate(flops=weight, bytes_accessed=2**18, transcendentals=0),
        name=name,
    )(*operands)


def shaped(*shape):
    return jax.ShapeDtypeStruct(shape, BF)


def column(block):
    return pl.ds(pl.multiple_of(block * 256, 256), 256)


def pack_kernel(acts, cot, out, sems):
    core = lax.axis_index("core")
    copies = [
        pltpu.make_async_copy(
            acts.at[:, column(2 * k + 1 - core)], out.at[:, 256 * k : 256 * k + 256], sems.at[k]
        )
        for k in range(8)
    ] + [pltpu.make_async_copy(cot, out.at[:, 2048:], sems.at[8])]
    for copy in copies:
        copy.start()
    for copy in copies:
        copy.wait()


def fold_kernel(weight, globe, momentum, *rest):
    out = rest[-1]
    row = lax.axis_index(REP) * 8
    share = share_of(globe[0, 0], momentum[0, 0]) / SCALE
    out[...] = weight[0]
    start = pl.multiple_of(row // 16 * 16, 16)
    half = lax.broadcasted_iota(jnp.int32, (2, 8, 512), 0) == lax.rem(row // 8, 2)
    put = jnp.where(half, share[None], 0.0).reshape(16, 512)
    out[pl.ds(start, 16), :] = (weight[0, pl.ds(start, 16), :].astype(F32) + put).astype(BF)


def spread_kernel(scale, parts, *rest):
    out = rest[-1]
    total = parts[0].astype(F32)
    for k in range(1, parts.shape[0]):
        total += parts[k].astype(F32)
    total = (scale * total).astype(BF)
    for k in range(out.shape[0]):
        out[k] = total


def term(acts, cot, other, block, half):
    dims = (((0,), (0,)), ((), ()))
    return lax.dot_general(
        acts[:, column(block)], cot[...], dims, preferred_element_type=F32
    ) + lax.dot_general(other[:, column(half)], other[:, 2048:], dims, preferred_element_type=F32)


def sent_kernel(acts, cot, other, *rest):
    out = rest[-1]
    core, yhi = lax.axis_index("core"), 1 - lax.axis_index("yhi")
    for x in range(4):
        out[x] = term(acts, cot, other, 4 * x + 2 * yhi + core, 2 * x + yhi).astype(BF)


def kept_kernel(acts, cot, other, came, *outs):
    core, yhi, x = (lax.axis_index(n) for n in ("core", "yhi", "x"))
    for shift, out in enumerate(outs):
        to = lax.rem(x + shift, 4)
        total = term(acts, cot, other, 4 * to + 2 * yhi + core, 2 * to + yhi)
        out[...] = (total + came[to].astype(F32)).astype(BF)


def input_kernel(cot, other, *refs):
    pairs, (own, mate) = refs[:4], refs[-2:]
    tokens = cot.shape[0]
    left = jnp.concatenate([cot[...], other[:, 2048:]], 0)
    x, yhi = lax.axis_index("x"), lax.axis_index("yhi")
    for shift in range(4):
        for k in range(2):
            spot = column(2 * lax.rem(x + 4 - shift, 4) + (yhi if k == 0 else 1 - yhi))
            both = lax.dot_general(
                left, pairs[shift][k], (((1,), (1,)), ((), ())), preferred_element_type=F32
            ).astype(BF)
            own[:, spot] = both[:tokens]
            mate[:, spot] = both[tokens:]


def join_kernel(own, mate, *rest):
    out = rest[-1]
    core = lax.axis_index("core")
    for k in range(8):
        out[:, column(2 * k + core)] = own[:, 256 * k : 256 * k + 256]
        out[:, column(2 * k + 1 - core)] = mate[:, 256 * k : 256 * k + 256]


def finish_kernel(t0, t1, t2, t3, weight, adam_first, adam_second, rows, *outs):
    new_weight, new_first, new_second = outs
    grads = t0[...].astype(F32) + t1[...].astype(F32) + t2[...].astype(F32) + t3[...].astype(F32)
    wide = weight[0].astype(F32)
    first = beta_first * adam_first[0].astype(F32) + (1.0 - beta_first) * grads
    second = beta_second * adam_second[0].astype(F32) + (1.0 - beta_second) * grads * grads
    first_hat = first / (1.0 - beta_first**STEP)
    second_hat = second / (1.0 - beta_second**STEP)
    adamw = wide - inner_rate * (
        first_hat / (jnp.sqrt(second_hat) + epsilon_adam) + decay_rate * wide
    )
    new_weight[0] = (mix_factor * adamw + (1.0 - mix_factor) * rows[...].astype(F32)).astype(BF)
    new_first[0] = first.astype(BF)
    new_second[0] = second.astype(BF)


def finish(terms, weight, adam_first, adam_second, rows):
    size = 64
    state = pl.BlockSpec((1, size, 512), lambda j: (0, j, 0))
    return pl.pallas_call(
        finish_kernel,
        grid=(256 // size,),
        in_specs=[
            *[pl.BlockSpec((size, 512), lambda j: (j, 0))] * 4,
            *[state] * 3,
            pl.BlockSpec((size, 512), lambda j: (j, 0)),
        ],
        out_specs=[state] * 3,
        out_shape=[jax.ShapeDtypeStruct((1, 256, 512), BF)] * 3,
        compiler_params=pltpu.CompilerParams(vmem_limit_bytes=16 * 2**20),
        cost_estimate=pl.CostEstimate(flops=0, bytes_accessed=2**18, transcendentals=0),
        name="adam_and_mix",
    )(*terms, weight, adam_first, adam_second, rows)


def shards(acts, cot, inner_weight, adam_first, adam_second, global_weight, outer_momentum):
    weight = inner_weight[0]
    tokens = acts.shape[0]

    across = permute(weight, "yhi", 2, 1)

    packed = call(
        pack_kernel,
        (acts, cot),
        shaped(tokens, 2560),
        "pack", limit=60,
        loose=2,
        scratch=[pltpu.SemaphoreType.DMA((9,))],
        space=pltpu.HBM,
    )
    other = permute(packed, "core", 2, 1)

    blocks = call(
        fold_kernel,
        (inner_weight, global_weight, outer_momentum),
        shaped(256, 512),
        "fold_outer_state",
    )
    near = ("ylo", "zlo")
    parts = lax.all_to_all(blocks.reshape(8, 32, 512), near, 0, 0, tiled=True)
    send = call(
        sent_kernel, (acts, cot, other, blocks, across), shaped(4, 256, 512), "sent_terms", loose=2
    )
    came = permute(send, "yhi", 2, 1)

    keep = call(kept_kernel, (acts, cot, other, came), [shaped(256, 512)] * 4, "kept_terms")
    terms = [keep[0]] + [permute(keep[s], "x", 4, s) for s in (1, 3, 2)]

    pair = jnp.stack([weight, across])
    pairs = [pair] + [permute(pair, "x", 4, s) for s in (1, 3, 2)]
    pairs = [pairs[0], pairs[1], pairs[3], pairs[2]]

    parts = call(functools.partial(spread_kernel, 1.0), (parts,), shaped(4, 32, 512), "near_sum", weight=2000000000)
    parts = lax.all_to_all(parts, "zhi", 0, 0, tiled=True)
    mine, sent = call(
        input_kernel,
        (cot, other, *pairs),
        [shaped(tokens, 2048)] * 2,
        "input_grad_columns",
        loose=0,
    )
    rows = call(
        functools.partial(spread_kernel, SCALE),
        (parts, terms[1], terms[2], terms[3], sent),
        shaped(8, 32, 512),
        "far_sum",
        loose=4,
    )
    rows = lax.all_to_all(rows, near, 0, 0, tiled=True).reshape(256, 512)

    globe, momentum = global_weight[0, 0], outer_momentum[0, 0]
    own = lax.dynamic_slice_in_dim(rows, lax.axis_index(REP) * 8, 8, 0).astype(F32)
    outer_delta = globe - (own - share_of(globe, momentum)) / (32 * SCALE)
    momentum_new = momentum_coef * momentum + outer_delta
    global_new = globe - outer_rate * (outer_delta + momentum_coef * momentum_new)

    mate = permute(sent, "core", 2, 1)
    input_grad = call(
        join_kernel, (mine, mate), shaped(tokens, 4096), "input_grad", loose=0
    )

    new_weight, new_first, new_second = finish(
        terms, inner_weight, adam_first, adam_second, rows
    )
    return (
        input_grad,
        new_weight,
        new_first,
        new_second,
        global_new[None, None],
        momentum_new[None, None],
    )


def solution(mesh):
    return jax.shard_map(
        shards,
        mesh=Mesh(mesh.devices.reshape(SIZES), AXES),
        in_specs=(
            P(REP + FSDP, None),
            P(REP + FSDP, None),
            P(REP, FSDP, None),
            P(REP, FSDP, None),
            P(REP, FSDP, None),
            P(FSDP, REP, None, None),
            P(FSDP, REP, None, None),
        ),
        out_specs=(
            P(REP + FSDP, None),
            P(REP, FSDP, None),
            P(REP, FSDP, None),
            P(REP, FSDP, None),
            P(FSDP, REP, None, None),
            P(FSDP, REP, None, None),
        ),
        check_vma=False,
    )
```

time: 351 us -> 93.1 us (0.27)
  the two profiles are of different devices: /device:TPU:2 before, /device:TPU:6 now
where the time goes in v1:
time: 93.1 us; the launch traced here: 92 us
  starting transfers between devices  58.5 us (63%)
  Pallas kernels  17.5 us (19%)
  waiting for transfers between devices  12.1 us (13%)
  other arithmetic  1.62 us (2%)
  local copies, waits for them, and re-layouts  1.38 us (1%)
    ppermute x10, starting transfers between devices, permute(): lax.ppermute(array, axis, [(i, (i + shift) % size) for i in range(size)])  34.8 us
    all_to_all x1, starting transfers between devices, shards(): parts = lax.all_to_all(parts, 'zhi', 0, 0, tiled=True)  14.3 us
    pallas_call x8, Pallas kernels, call(): pl.pallas_call(kernel, in_specs=[pl.BlockSpec(memory_space=pltpu.VMEM)] *...  14 us
    ppermute x10, waiting for transfers between devices, permute(): lax.ppermute(array, axis, [(i, (i + shift) % size) for i in range(size)])  9.08 us
    all_to_all x1, starting transfers between devices, shards(): parts = lax.all_to_all(blocks.reshape(8, 32, 512), near, 0, 0, tiled=True)  6.01 us
    pallas_call x1, Pallas kernels, finish(): pl.pallas_call(finish_kernel, grid=(256 // size,), in_specs=[*[pl.BlockSp...  3.5 us
    all_to_all x1, starting transfers between devices, shards(): rows = lax.all_to_all(rows, near, 0, 0, tiled=True).reshape(256, 512)  3.43 us
    all_to_all x1, waiting for transfers between devices, shards(): rows = lax.all_to_all(rows, near, 0, 0, tiled=True).reshape(256, 512)  3.04 us
  transfers between devices with their start and end apart: 13, of which 4 were waited for; matrix products, arithmetic and copies ran while one was open for 1% of the time, Pallas kernels for 11%

profile of v1, /device:TPU:6, one launch (start us, length us, event | category | flops | bytes accessed | tf_op | source)
XLA Modules:
  0.0 92.0 jit_solution(14724825613037152950)
XLA Ops:
  0.6 0.0 copy-start
  0.6 0.0 copy-start.1
  0.7 0.0 copy-start.2
  0.7 0.0 copy-start.9
  0.7 0.0 copy-start.10
  0.7 2.4 %pack.1 = bf16[192,2560]{1,0:T(8,128)(2,1)} custom-call(bf16[192,4096]{1,0:T(8,128)(2,1)} %acts.5, bf16[192,512]{1,0:T(8,128)(2,1)} %cot.7), custom_call_target="tpu_custom_call" | custom-call | bytes 262144 | tf_op jit(solution)/shard_map/pack/pallas_call | solution.py:44
  3.1 1.9 %collective-permute-start = (bf16[192,2560]{1,0:T(8,128)(2,1)}, bf16[192,2560]{1,0:T(8,128)(2,1)S(1)}, u32[]{:S(2)}, u32[]{:S(2)}) collective-permute-start(bf16[192,2560]{1,0:T(8,128)(2,1)} %pack.1), channel_id=1, source_target_pairs={{0,1},{1,0},{2,3},{3,2},{4,5},{5,4},{6,7},{7,6},{8,9},{9,8},{10,11... | collective-permute-start | bytes 2949128 | tf_op jit(solution)/shard_map/ppermute | solution.py:30
  5.1 0.0 copy-done.2
  5.1 5.1 %collective-permute-start.1 = (bf16[256,512]{1,0:T(8,128)(2,1)S(1)}, bf16[256,512]{1,0:T(8,128)(2,1)S(1)}, u32[]{:S(2)}, u32[]{:S(2)}) collective-permute-start(bf16[256,512]{1,0:T(8,128)(2,1)S(1)} %bitcast.46), channel_id=1, source_target_pairs={{0,2},{2,0},{1,3},{3,1},{4,6},{6,4},{5,7},{7,5},{8,10},{10,8},{9,1... | collective-permute-start | bytes 786440 | tf_op jit(solution)/shard_map/ppermute | solution.py:30
  10.2 0.0 copy-done.9
  10.2 0.0 copy-done.10
  10.2 0.7 fold_outer_state.1.rest_0_
  10.9 6.0 %all-to-all-start = ((bf16[8,32,512]{2,1,0:T(8,128)(2,1)}), bf16[8,32,512]{2,1,0:T(8,128)(2,1)}, u32[]{:S(2)}, u32[]{:S(2)}) async-start(bf16[8,32,512]{2,1,0:T(8,128)(2,1)} %bitcast.2), calls=%async_computation | async-start | bytes 524288 | tf_op jit(solution)/shard_map/all_to_all | solution.py:203
  17.0 0.2 collective-permute-done.1.rest_1_
  17.2 0.0 copy-start.3
  17.2 0.0 collective-permute-done.other
  17.2 0.0 copy-done
  17.2 0.0 copy-done.1
  17.2 1.7 %sent_terms.1 = bf16[4,256,512]{2,1,0:T(8,128)(2,1)} custom-call(bf16[192,4096]{1,0:T(8,128)(2,1)S(1)} %copy-done, bf16[192,512]{1,0:T(8,128)(2,1)S(1)} %copy-done.1, bf16[192,2560]{1,0:T(8,128)(2,1)S(1)} %collective-permute-done.other, bf16[256,512]{1,0:T(8,128)(2,1)} %fold_outer_state.1.rest_0_, bf16[256,512]{1,0:T(8,128)(2,1)S(1)} %collective-permute-done.1.rest_1_), custom_call_target="tpu_custom_call" | custom-call | bytes 262144 | tf_op jit(solution)/shard_map/sent_terms/pallas_call | solution.py:44
  18.9 0.0 copy-done.3
  18.9 5.1 %collective-permute-start.6 = (bf16[4,256,512]{2,1,0:T(8,128)(2,1)}, bf16[4,256,512]{2,1,0:T(8,128)(2,1)}, u32[]{:S(2)}, u32[]{:S(2)}) collective-permute-start(bf16[4,256,512]{2,1,0:T(8,128)(2,1)} %sent_terms.1), channel_id=1, source_target_pairs={{0,2},{2,0},{1,3},{3,1},{4,6},{6,4},{5,7},{7,5},{8,10},{10,8},{9,1... | collective-permute-start | bytes 3145736 | tf_op jit(solution)/shard_map/ppermute | solution.py:30
  24.0 1.0 %pad_maximum_fusion.refs_0_ = bf16[2,256,512]{2,1,0:T(8,128)(2,1)S(1)} fusion(bf16[1,256,512]{2,1,0:T(8,128)(2,1)} %bitcast.49, bf16[1,256,512]{2,1,0:T(8,128)(2,1)S(1)} %copy-done.2), kind=kLoop, calls=%fused_computation | loop fusion | flops 262144 | bytes 1048576 | tf_op jit(solution)/shard_map/stack | solution.py:212
  25.0 5.0 %collective-permute-start.2 = (bf16[2,256,512]{2,1,0:T(8,128)(2,1)S(1)}, bf16[2,256,512]{2,1,0:T(8,128)(2,1)}, u32[]{:S(2)}, u32[]{:S(2)}) collective-permute-start(bf16[2,256,512]{2,1,0:T(8,128)(2,1)S(1)} %pad_maximum_fusion.refs_0_), channel_id=1, source_target_pairs={{0,4},{4,8},{8,12},{12,0},{1,5},{5,9},{9,13},{13,1},{2,6},{6,10},{... | collective-permute-start | bytes 1572872 | tf_op jit(solution)/shard_map/ppermute | solution.py:30
  30.1 1.9 %collective-permute-start.3 = (bf16[2,256,512]{2,1,0:T(8,128)(2,1)S(1)}, bf16[2,256,512]{2,1,0:T(8,128)(2,1)}, u32[]{:S(2)}, u32[]{:S(2)}) collective-permute-start(bf16[2,256,512]{2,1,0:T(8,128)(2,1)S(1)} %pad_maximum_fusion.refs_0_), channel_id=1, source_target_pairs={{0,8},{4,12},{8,0},{12,4},{1,9},{5,13},{9,1},{13,5},{2,10},{6,14},... | collective-permute-start | bytes 1572872 | tf_op jit(solution)/shard_map/ppermute | solution.py:30
  32.0 2.8 %collective-permute-start.4 = (bf16[2,256,512]{2,1,0:T(8,128)(2,1)S(1)}, bf16[2,256,512]{2,1,0:T(8,128)(2,1)}, u32[]{:S(2)}, u32[]{:S(2)}) collective-permute-start(bf16[2,256,512]{2,1,0:T(8,128)(2,1)S(1)} %pad_maximum_fusion.refs_0_), channel_id=1, source_target_pairs={{0,12},{4,0},{8,4},{12,8},{1,13},{5,1},{9,5},{13,9},{2,14},{6,2},{... | collective-permute-start | bytes 1572872 | tf_op jit(solution)/shard_map/ppermute | solution.py:30
  34.8 0.0 all-to-all-done.parts
  34.8 1.0 %near_sum.1 = bf16[4,32,512]{2,1,0:T(8,128)(2,1)S(1)} custom-call(bf16[8,32,512]{2,1,0:T(8,128)(2,1)} %all-to-all-done.parts), custom_call_target="tpu_custom_call" | custom-call | flops 2000000000 | bytes 262144 | tf_op jit(solution)/shard_map/near_sum/pallas_call | solution.py:44
  35.8 0.0 copy-start.8
  35.8 0.6 copy-done.8
  36.5 14.3 %all-to-all-start.1 = ((bf16[4,32,512]{2,1,0:T(8,128)(2,1)}), bf16[4,32,512]{2,1,0:T(8,128)(2,1)}, u32[]{:S(2)}, u32[]{:S(2)}) async-start(bf16[4,32,512]{2,1,0:T(8,128)(2,1)} %copy-done.8), calls=%async_computation.1 | async-start | bytes 262144 | tf_op jit(solution)/shard_map/all_to_all | solution.py:217
  50.8 0.0 collective-permute-done.6.came
  50.8 2.7 %kept_terms.1 = (bf16[256,512]{1,0:T(8,128)(2,1)S(1)}, bf16[256,512]{1,0:T(8,128)(2,1)}, bf16[256,512]{1,0:T(8,128)(2,1)}, bf16[256,512]{1,0:T(8,128)(2,1)}) custom-call(bf16[192,4096]{1,0:T(8,128)(2,1)S(1)} %copy-done, bf16[192,512]{1,0:T(8,128)(2,1)S(1)} %copy-done.1, bf16[192,2560]{1,0:T(8,128)(2,1)S(1)} %collective-permute-done.other, ...), custom_call_target="tpu_custom_call" | custom-call | bytes 262144 | tf_op jit(solution)/shard_map/kept_terms/pallas_call | solution.py:44
  53.5 0.0 copy-start.6
  53.5 0.7 copy-done.6
  54.2 5.1 %collective-permute-start.7 = (bf16[256,512]{1,0:T(8,128)(2,1)}, bf16[256,512]{1,0:T(8,128)(2,1)}, u32[]{:S(2)}, u32[]{:S(2)}) collective-permute-start(bf16[256,512]{1,0:T(8,128)(2,1)} %get-tuple-element.18), channel_id=1, source_target_pairs={{0,4},{4,8},{8,12},{12,0},{1,5},{5,9},{9,13},{13,1},{2,6},{6,10},{... | collective-permute-start | bytes 786440 | tf_op jit(solution)/shard_map/ppermute | solution.py:30
  59.3 1.9 %collective-permute-start.8 = (bf16[256,512]{1,0:T(8,128)(2,1)}, bf16[256,512]{1,0:T(8,128)(2,1)}, u32[]{:S(2)}, u32[]{:S(2)}) collective-permute-start(bf16[256,512]{1,0:T(8,128)(2,1)} %get-tuple-element.19), channel_id=1, source_target_pairs={{0,12},{4,0},{8,4},{12,8},{1,13},{5,1},{9,5},{13,9},{2,14},{6,2},{... | collective-permute-start | bytes 786440 | tf_op jit(solution)/shard_map/ppermute | solution.py:30
  61.3 0.0 collective-permute-done.2.refs_1_
  61.3 3.9 %collective-permute-start.9 = (bf16[256,512]{1,0:T(8,128)(2,1)}, bf16[256,512]{1,0:T(8,128)(2,1)}, u32[]{:S(2)}, u32[]{:S(2)}) collective-permute-start(bf16[256,512]{1,0:T(8,128)(2,1)} %get-tuple-element.20), channel_id=1, source_target_pairs={{0,8},{4,12},{8,0},{12,4},{1,9},{5,13},{9,1},{13,5},{2,10},{6,14},... | collective-permute-start | bytes 786440 | tf_op jit(solution)/shard_map/ppermute | solution.py:30
  65.2 0.0 collective-permute-done.3.refs_2_
  65.2 0.0 collective-permute-done.4.refs_3_
  65.2 2.4 %input_grad_columns.1 = (bf16[192,2048]{1,0:T(8,128)(2,1)S(1)}, bf16[192,2048]{1,0:T(8,128)(2,1)S(1)}) custom-call(bf16[192,512]{1,0:T(8,128)(2,1)S(1)} %copy-done.1, bf16[192,2560]{1,0:T(8,128)(2,1)S(1)} %collective-permute-done.other, bf16[2,256,512]{2,1,0:T(8,128)(2,1)S(1)} %pad_maximum_fusion.refs_0_, ...), custom_call_target="tpu_custom_call" | custom-call | bytes 262144 | tf_op jit(solution)/shard_map/input_grad_columns/pallas_call | solution.py:44
  67.6 0.0 all-to-all-done.1.parts
  67.7 0.0 collective-permute-done.7.rest_0_.t1
  67.7 6.6 %collective-permute-done.8.rest_1_.t2 = bf16[256,512]{1,0:T(8,128)(2,1)} collective-permute-done((bf16[256,512]{1,0:T(8,128)(2,1)}, bf16[256,512]{1,0:T(8,128)(2,1)}, u32[]{:S(2)}, u32[]{:S(2)}) %collective-permute-start.8) | collective-permute-done | bytes 262176 | tf_op jit(solution)/shard_map/ppermute | solution.py:30
  74.3 0.0 collective-permute-done.9.rest_2_.t3
  74.3 1.6 %far_sum.1 = bf16[8,32,512]{2,1,0:T(8,128)(2,1)} custom-call(bf16[4,32,512]{2,1,0:T(8,128)(2,1)} %all-to-all-done.1.parts, bf16[256,512]{1,0:T(8,128)(2,1)} %collective-permute-done.7.rest_0_.t1, bf16[256,512]{1,0:T(8,128)(2,1)} %collective-permute-done.8.rest_1_.t2, bf16[256,512]{1,0:T(8,128)(2,1)} %collective-permute-done.9.rest_2_.t3, ...), custom_call_target="tpu_custom_call" | custom-call | bytes 262144 | tf_op jit(solution)/shard_map/far_sum/pallas_call | solution.py:44
  75.9 3.4 %all-to-all-start.2 = ((bf16[8,32,512]{2,1,0:T(8,128)(2,1)}), bf16[8,32,512]{2,1,0:T(8,128)(2,1)S(1)}, u32[]{:S(2)}, u32[]{:S(2)}) async-start(bf16[8,32,512]{2,1,0:T(8,128)(2,1)} %far_sum.1), calls=%async_computation.2 | async-start | bytes 524288 | tf_op jit(solution)/shard_map/all_to_all | solution.py:232
  79.3 1.9 %collective-permute-start.5 = (bf16[192,2048]{1,0:T(8,128)(2,1)S(1)}, bf16[192,2048]{1,0:T(8,128)(2,1)S(1)}, u32[]{:S(2)}, u32[]{:S(2)}) collective-permute-start(bf16[192,2048]{1,0:T(8,128)(2,1)S(1)} %get-tuple-element.16.rest_3_), channel_id=1, source_target_pairs={{0,1},{1,0},{2,3},{3,2},{4,5},{5,4},{6,7},{7,6},{8,9},{9,8},{10,11... | collective-permute-start | bytes 2359304 | tf_op jit(solution)/shard_map/ppermute | solution.py:30
  81.3 2.2 %collective-permute-done.5.mate = bf16[192,2048]{1,0:T(8,128)(2,1)S(1)} collective-permute-done((bf16[192,2048]{1,0:T(8,128)(2,1)S(1)}, bf16[192,2048]{1,0:T(8,128)(2,1)S(1)}, u32[]{:S(2)}, u32[]{:S(2)}) %collective-permute-start.5) | collective-permute-done | bytes 786464 | tf_op jit(solution)/shard_map/ppermute | solution.py:30
  83.5 0.0 copy-start.11
  83.5 0.0 copy-start.4
  83.5 0.0 copy-start.5
  83.5 0.0 copy-start.7
  83.5 1.3 %input_grad.1 = bf16[192,4096]{1,0:T(8,128)(2,1)} custom-call(bf16[192,2048]{1,0:T(8,128)(2,1)S(1)} %get-tuple-element.15.own, bf16[192,2048]{1,0:T(8,128)(2,1)S(1)} %collective-permute-done.5.mate), custom_call_target="tpu_custom_call" | custom-call | bytes 262144 | tf_op jit(solution)/shard_map/input_grad/pallas_call | solution.py:44
  84.9 3.0 %all-to-all-done.2 = bf16[8,32,512]{2,1,0:T(8,128)(2,1)S(1)} async-done(((bf16[8,32,512]{2,1,0:T(8,128)(2,1)}), bf16[8,32,512]{2,1,0:T(8,128)(2,1)S(1)}, u32[]{:S(2)}, u32[]{:S(2)}) %all-to-all-start.2) | async-done | bytes 262176 | tf_op jit(solution)/shard_map/all_to_all | solution.py:232
  87.9 0.0 copy-done.11
  87.9 0.6 fusion.4
  88.5 0.0 copy-done.4
  88.5 0.0 copy-done.5
  88.5 0.0 copy-done.7
  88.5 3.5 %adam_and_mix.1 = (bf16[1,256,512]{2,1,0:T(8,128)(2,1)}, bf16[1,256,512]{2,1,0:T(8,128)(2,1)}, bf16[1,256,512]{2,1,0:T(8,128)(2,1)}) custom-call(bf16[256,512]{1,0:T(8,128)(2,1)S(1)} %copy-done.7, bf16[256,512]{1,0:T(8,128)(2,1)} %collective-permute-done.7.rest_0_.t1, bf16[256,512]{1,0:T(8,128)(2,1)} %collective-permute-done.8.rest_1_.t2, ...), custom_call_target="tpu_custom_call" | custom-call | bytes 262144 | tf_op jit(solution)/shard_map/adam_and_mix/pallas_call | solution.py:163
Async XLA Ops:
  0.6 16.6 %copy-start = (bf16[192,4096]{1,0:T(8,128)(2,1)S(1)}, bf16[192,4096]{1,0:T(8,128)(2,1)}, u32[]{:S(2)}) copy-start(bf16[192,4096]{1,0:T(8,128)(2,1)} %acts.5) | copy-start | bytes 4718596
  0.6 16.6 %copy-start.1 = (bf16[192,512]{1,0:T(8,128)(2,1)S(1)}, bf16[192,512]{1,0:T(8,128)(2,1)}, u32[]{:S(2)}) copy-start(bf16[192,512]{1,0:T(8,128)(2,1)} %cot.7) | copy-start | bytes 589828
  0.7 4.4 %copy-start.2 = (bf16[1,256,512]{2,1,0:T(8,128)(2,1)S(1)}, bf16[1,256,512]{2,1,0:T(8,128)(2,1)}, u32[]{:S(2)}) copy-start(bf16[1,256,512]{2,1,0:T(8,128)(2,1)} %weight.3) | copy-start | bytes 786436
  0.7 9.5 %copy-start.9 = (f32[1,1,8,512]{3,2,1,0:T(8,128)S(1)}, f32[1,1,8,512]{3,2,1,0:T(8,128)}, u32[]{:S(2)}) copy-start(f32[1,1,8,512]{3,2,1,0:T(8,128)} %globe.1) | copy-start | bytes 49156
  0.7 9.5 %copy-start.10 = (f32[1,1,8,512]{3,2,1,0:T(8,128)S(1)}, f32[1,1,8,512]{3,2,1,0:T(8,128)}, u32[]{:S(2)}) copy-start(f32[1,1,8,512]{3,2,1,0:T(8,128)} %momentum.1) | copy-start | bytes 49156
  3.1 14.1 %collective-permute-start = (bf16[192,2560]{1,0:T(8,128)(2,1)}, bf16[192,2560]{1,0:T(8,128)(2,1)S(1)}, u32[]{:S(2)}, u32[]{:S(2)}) collective-permute-start(bf16[192,2560]{1,0:T(8,128)(2,1)} %pack.1), channel_id=1, source_target_pairs={{0,1},{1,0},{2,3},{3,2},{4,5},{5,4},{6,7},{7,6},{8,9},{9,8},{10,11... | collective-permute-start | bytes 2949128 | tf_op jit(solution)/shard_map/ppermute | solution.py:30
  5.1 12.1 %collective-permute-start.1 = (bf16[256,512]{1,0:T(8,128)(2,1)S(1)}, bf16[256,512]{1,0:T(8,128)(2,1)S(1)}, u32[]{:S(2)}, u32[]{:S(2)}) collective-permute-start(bf16[256,512]{1,0:T(8,128)(2,1)S(1)} %bitcast.46), channel_id=1, source_target_pairs={{0,2},{2,0},{1,3},{3,1},{4,6},{6,4},{5,7},{7,5},{8,10},{10,8},{9,1... | collective-permute-start | bytes 786440 | tf_op jit(solution)/shard_map/ppermute | solution.py:30
  10.9 23.9 %all-to-all-start = ((bf16[8,32,512]{2,1,0:T(8,128)(2,1)}), bf16[8,32,512]{2,1,0:T(8,128)(2,1)}, u32[]{:S(2)}, u32[]{:S(2)}) async-start(bf16[8,32,512]{2,1,0:T(8,128)(2,1)} %bitcast.2), calls=%async_computation | async-start | bytes 524288 | tf_op jit(solution)/shard_map/all_to_all | solution.py:203
  17.2 1.8 %copy-start.3 = (bf16[256,512]{1,0:T(8,128)(2,1)}, bf16[256,512]{1,0:T(8,128)(2,1)S(1)}, u32[]{:S(2)}) copy-start(bf16[256,512]{1,0:T(8,128)(2,1)S(1)} %collective-permute-done.1.rest_1_) | copy-start | bytes 786436
  18.9 31.9 %collective-permute-start.6 = (bf16[4,256,512]{2,1,0:T(8,128)(2,1)}, bf16[4,256,512]{2,1,0:T(8,128)(2,1)}, u32[]{:S(2)}, u32[]{:S(2)}) collective-permute-start(bf16[4,256,512]{2,1,0:T(8,128)(2,1)} %sent_terms.1), channel_id=1, source_target_pairs={{0,2},{2,0},{1,3},{3,1},{4,6},{6,4},{5,7},{7,5},{8,10},{10,8},{9,1... | collective-permute-start | bytes 3145736 | tf_op jit(solution)/shard_map/ppermute | solution.py:30
  25.0 36.2 %collective-permute-start.2 = (bf16[2,256,512]{2,1,0:T(8,128)(2,1)S(1)}, bf16[2,256,512]{2,1,0:T(8,128)(2,1)}, u32[]{:S(2)}, u32[]{:S(2)}) collective-permute-start(bf16[2,256,512]{2,1,0:T(8,128)(2,1)S(1)} %pad_maximum_fusion.refs_0_), channel_id=1, source_target_pairs={{0,4},{4,8},{8,12},{12,0},{1,5},{5,9},{9,13},{13,1},{2,6},{6,10},{... | collective-permute-start | bytes 1572872 | tf_op jit(solution)/shard_map/ppermute | solution.py:30
  30.1 35.1 %collective-permute-start.3 = (bf16[2,256,512]{2,1,0:T(8,128)(2,1)S(1)}, bf16[2,256,512]{2,1,0:T(8,128)(2,1)}, u32[]{:S(2)}, u32[]{:S(2)}) collective-permute-start(bf16[2,256,512]{2,1,0:T(8,128)(2,1)S(1)} %pad_maximum_fusion.refs_0_), channel_id=1, source_target_pairs={{0,8},{4,12},{8,0},{12,4},{1,9},{5,13},{9,1},{13,5},{2,10},{6,14},... | collective-permute-start | bytes 1572872 | tf_op jit(solution)/shard_map/ppermute | solution.py:30
  32.0 33.2 %collective-permute-start.4 = (bf16[2,256,512]{2,1,0:T(8,128)(2,1)S(1)}, bf16[2,256,512]{2,1,0:T(8,128)(2,1)}, u32[]{:S(2)}, u32[]{:S(2)}) collective-permute-start(bf16[2,256,512]{2,1,0:T(8,128)(2,1)S(1)} %pad_maximum_fusion.refs_0_), channel_id=1, source_target_pairs={{0,12},{4,0},{8,4},{12,8},{1,13},{5,1},{9,5},{13,9},{2,14},{6,2},{... | collective-permute-start | bytes 1572872 | tf_op jit(solution)/shard_map/ppermute | solution.py:30
  35.8 0.6 copy-start.8
  36.5 31.2 %all-to-all-start.1 = ((bf16[4,32,512]{2,1,0:T(8,128)(2,1)}), bf16[4,32,512]{2,1,0:T(8,128)(2,1)}, u32[]{:S(2)}, u32[]{:S(2)}) async-start(bf16[4,32,512]{2,1,0:T(8,128)(2,1)} %copy-done.8), calls=%async_computation.1 | async-start | bytes 262144 | tf_op jit(solution)/shard_map/all_to_all | solution.py:217
  53.5 0.7 copy-start.6
  54.2 13.5 %collective-permute-start.7 = (bf16[256,512]{1,0:T(8,128)(2,1)}, bf16[256,512]{1,0:T(8,128)(2,1)}, u32[]{:S(2)}, u32[]{:S(2)}) collective-permute-start(bf16[256,512]{1,0:T(8,128)(2,1)} %get-tuple-element.18), channel_id=1, source_target_pairs={{0,4},{4,8},{8,12},{12,0},{1,5},{5,9},{9,13},{13,1},{2,6},{6,10},{... | collective-permute-start | bytes 786440 | tf_op jit(solution)/shard_map/ppermute | solution.py:30
  59.3 14.9 %collective-permute-start.8 = (bf16[256,512]{1,0:T(8,128)(2,1)}, bf16[256,512]{1,0:T(8,128)(2,1)}, u32[]{:S(2)}, u32[]{:S(2)}) collective-permute-start(bf16[256,512]{1,0:T(8,128)(2,1)} %get-tuple-element.19), channel_id=1, source_target_pairs={{0,12},{4,0},{8,4},{12,8},{1,13},{5,1},{9,5},{13,9},{2,14},{6,2},{... | collective-permute-start | bytes 786440 | tf_op jit(solution)/shard_map/ppermute | solution.py:30
  61.3 13.0 %collective-permute-start.9 = (bf16[256,512]{1,0:T(8,128)(2,1)}, bf16[256,512]{1,0:T(8,128)(2,1)}, u32[]{:S(2)}, u32[]{:S(2)}) collective-permute-start(bf16[256,512]{1,0:T(8,128)(2,1)} %get-tuple-element.20), channel_id=1, source_target_pairs={{0,8},{4,12},{8,0},{12,4},{1,9},{5,13},{9,1},{13,5},{2,10},{6,14},... | collective-permute-start | bytes 786440 | tf_op jit(solution)/shard_map/ppermute | solution.py:30
  75.9 12.0 %all-to-all-start.2 = ((bf16[8,32,512]{2,1,0:T(8,128)(2,1)}), bf16[8,32,512]{2,1,0:T(8,128)(2,1)S(1)}, u32[]{:S(2)}, u32[]{:S(2)}) async-start(bf16[8,32,512]{2,1,0:T(8,128)(2,1)} %far_sum.1), calls=%async_computation.2 | async-start | bytes 524288 | tf_op jit(solution)/shard_map/all_to_all | solution.py:232
  79.3 4.2 %collective-permute-start.5 = (bf16[192,2048]{1,0:T(8,128)(2,1)S(1)}, bf16[192,2048]{1,0:T(8,128)(2,1)S(1)}, u32[]{:S(2)}, u32[]{:S(2)}) collective-permute-start(bf16[192,2048]{1,0:T(8,128)(2,1)S(1)} %get-tuple-element.16.rest_3_), channel_id=1, source_target_pairs={{0,1},{1,0},{2,3},{3,2},{4,5},{5,4},{6,7},{7,6},{8,9},{9,8},{10,11... | collective-permute-start | bytes 2359304 | tf_op jit(solution)/shard_map/ppermute | solution.py:30
  83.5 4.4 %copy-start.11 = (f32[1,1,8,512]{3,2,1,0:T(8,128)S(1)}, f32[1,1,8,512]{3,2,1,0:T(8,128)}, u32[]{:S(2)}) copy-start(f32[1,1,8,512]{3,2,1,0:T(8,128)} %momentum.1) | copy-start | bytes 49156
  83.5 5.0 %copy-start.4 = (bf16[1,256,512]{2,1,0:T(8,128)(2,1)S(1)}, bf16[1,256,512]{2,1,0:T(8,128)(2,1)}, u32[]{:S(2)}) copy-start(bf16[1,256,512]{2,1,0:T(8,128)(2,1)} %adam_first.1) | copy-start | bytes 786436
  83.5 5.0 %copy-start.5 = (bf16[1,256,512]{2,1,0:T(8,128)(2,1)S(1)}, bf16[1,256,512]{2,1,0:T(8,128)(2,1)}, u32[]{:S(2)}) copy-start(bf16[1,256,512]{2,1,0:T(8,128)(2,1)} %adam_second.1) | copy-start | bytes 786436
  83.5 5.0 %copy-start.7 = (bf16[256,512]{1,0:T(8,128)(2,1)S(1)}, bf16[256,512]{1,0:T(8,128)(2,1)}, u32[]{:S(2)}) copy-start(bf16[256,512]{1,0:T(8,128)(2,1)} %copy-done.6) | copy-start | bytes 786436

commit v2 on v1

--- a/solution.py
+++ b/solution.py
@@ -141,8 +141,7 @@
         out[:, column(2 * k + 1 - core)] = mate[:, 256 * k : 256 * k + 256]
 
 
-def finish_kernel(t0, t1, t2, t3, weight, adam_first, adam_second, rows, *outs):
-    new_weight, new_first, new_second = outs
+def adam_kernel(t0, t1, t2, t3, weight, adam_first, adam_second, half, new_first, new_second):
     grads = t0[...].astype(F32) + t1[...].astype(F32) + t2[...].astype(F32) + t3[...].astype(F32)
     wide = weight[0].astype(F32)
     first = beta_first * adam_first[0].astype(F32) + (1.0 - beta_first) * grads
@@ -152,28 +151,21 @@
     adamw = wide - inner_rate * (
         first_hat / (jnp.sqrt(second_hat) + epsilon_adam) + decay_rate * wide
     )
-    new_weight[0] = (mix_factor * adamw + (1.0 - mix_factor) * rows[...].astype(F32)).astype(BF)
+    half[...] = mix_factor * adamw
     new_first[0] = first.astype(BF)
     new_second[0] = second.astype(BF)
 
 
-def finish(terms, weight, adam_first, adam_second, rows):
-    size = 64
-    state = pl.BlockSpec((1, size, 512), lambda j: (0, j, 0))
-    return pl.pallas_call(
-        finish_kernel,
-        grid=(256 // size,),
-        in_specs=[
-            *[pl.BlockSpec((size, 512), lambda j: (j, 0))] * 4,
-            *[state] * 3,
-            pl.BlockSpec((size, 512), lambda j: (j, 0)),
-        ],
-        out_specs=[state] * 3,
-        out_shape=[jax.ShapeDtypeStruct((1, 256, 512), BF)] * 3,
-        compiler_params=pltpu.CompilerParams(vmem_limit_bytes=16 * 2**20),
-        cost_estimate=pl.CostEstimate(flops=0, bytes_accessed=2**18, transcendentals=0),
-        name="adam_and_mix",
-    )(*terms, weight, adam_first, adam_second, rows)
+def mix_kernel(half, rows, globe, momentum, new_weight, new_global, new_momentum):
+    new_weight[0] = (half[...] + (1.0 - mix_factor) * rows[...].astype(F32)).astype(BF)
+
+    row = lax.axis_index(REP)
+    two = rows[pl.ds(pl.multiple_of(row // 2 * 16, 16), 16), :].astype(F32).reshape(2, 8, 512)
+    own = jnp.where(lax.rem(row, 2) == 0, two[0], two[1])
+    outer_delta = globe[0, 0] - (own - share_of(globe[0, 0], momentum[0, 0])) / (32 * SCALE)
+    momentum_new = momentum_coef * momentum[0, 0] + outer_delta
+    new_global[0, 0] = globe[0, 0] - outer_rate * (outer_delta + momentum_coef * momentum_new)
+    new_momentum[0, 0] = momentum_new
 
 
 def shards(acts, cot, inner_weight, adam_first, adam_second, global_weight, outer_momentum):
@@ -202,57 +194,54 @@
     near = ("ylo", "zlo")
     parts = lax.all_to_all(blocks.reshape(8, 32, 512), near, 0, 0, tiled=True)
     send = call(
-        sent_kernel, (acts, cot, other, blocks, across), shaped(4, 256, 512), "sent_terms", loose=2
+        sent_kernel, (acts, cot, other, across), shaped(4, 256, 512), "sent_terms", weight=2000000000, loose=1
     )
     came = permute(send, "yhi", 2, 1)
 
-    keep = call(kept_kernel, (acts, cot, other, came), [shaped(256, 512)] * 4, "kept_terms")
+    keep = call(kept_kernel, (acts, cot, other, came), [shaped(256, 512)] * 4, "kept_terms", weight=1000000000)
     terms = [keep[0]] + [permute(keep[s], "x", 4, s) for s in (1, 3, 2)]
 
     pair = jnp.stack([weight, across])
     pairs = [pair] + [permute(pair, "x", 4, s) for s in (1, 3, 2)]
     pairs = [pairs[0], pairs[1], pairs[3], pairs[2]]
 
-    parts = call(functools.partial(spread_kernel, 1.0), (parts,), shaped(4, 32, 512), "near_sum", weight=2000000000)
+    parts = call(functools.partial(spread_kernel, 1.0), (parts,), shaped(4, 32, 512), "near_sum", weight=1000000000)
     parts = lax.all_to_all(parts, "zhi", 0, 0, tiled=True)
     mine, sent = call(
         input_kernel,
-        (cot, other, *pairs),
+        (cot, other, *pairs, keep[0]),
         [shaped(tokens, 2048)] * 2,
         "input_grad_columns",
-        loose=0,
+        loose=1,
     )
     rows = call(
         functools.partial(spread_kernel, SCALE),
-        (parts, terms[1], terms[2], terms[3], sent),
+        (parts, sent),
         shaped(8, 32, 512),
         "far_sum",
-        loose=4,
+        loose=1,
     )
     rows = lax.all_to_all(rows, near, 0, 0, tiled=True).reshape(256, 512)
-
-    globe, momentum = global_weight[0, 0], outer_momentum[0, 0]
-    own = lax.dynamic_slice_in_dim(rows, lax.axis_index(REP) * 8, 8, 0).astype(F32)
-    outer_delta = globe - (own - share_of(globe, momentum)) / (32 * SCALE)
-    momentum_new = momentum_coef * momentum + outer_delta
-    global_new = globe - outer_rate * (outer_delta + momentum_coef * momentum_new)
 
     mate = permute(sent, "core", 2, 1)
     input_grad = call(
-        join_kernel, (mine, mate), shaped(tokens, 4096), "input_grad", loose=0
-    )
-
-    new_weight, new_first, new_second = finish(
-        terms, inner_weight, adam_first, adam_second, rows
-    )
-    return (
-        input_grad,
-        new_weight,
-        new_first,
-        new_second,
-        global_new[None, None],
-        momentum_new[None, None],
-    )
+        join_kernel, (mine, mate), shaped(tokens, 4096), "input_grad", weight=500000000, loose=0
+    )
+
+    half, new_first, new_second = call(
+        adam_kernel,
+        (*terms, inner_weight, adam_first, adam_second),
+        [jax.ShapeDtypeStruct((256, 512), F32)] + [shaped(1, 256, 512)] * 2,
+        "adam", weight=8000000000,
+    )
+    outer = jax.ShapeDtypeStruct((1, 1, 8, 512), F32)
+    new_weight, new_global, new_momentum = call(
+        mix_kernel,
+        (half, rows, global_weight, outer_momentum),
+        [shaped(1, 256, 512), outer, outer],
+        "mix", weight=500000000,
+    )
+    return input_grad, new_weight, new_first, new_second, new_global, new_momentum
 
 
 def solution(mesh):

time: 93.1 us -> 84.2 us (0.904)
  the two profiles are of different devices: /device:TPU:6 before, /device:TPU:4 now
where the time goes in v2:
time: 84.2 us; the launch traced here: 83.3 us
  starting transfers between devices  59.8 us (71%)
  Pallas kernels  17 us (20%)
  waiting for transfers between devices  3.24 us (4%)
  local copies, waits for them, and re-layouts  1.38 us (2%)
  other arithmetic  1 us (1%)
  between operations  0.92 us (1%)
    ppermute x10, starting transfers between devices, permute(): lax.ppermute(array, axis, [(i, (i + shift) % size) for i in range(size)])  37.6 us
    pallas_call x10, Pallas kernels, call(): pl.pallas_call(kernel, in_specs=[pl.BlockSpec(memory_space=pltpu.VMEM)] *...  17 us
    all_to_all x1, starting transfers between devices, shards(): parts = lax.all_to_all(parts, 'zhi', 0, 0, tiled=True)  12.8 us
    all_to_all x1, starting transfers between devices, shards(): parts = lax.all_to_all(blocks.reshape(8, 32, 512), near, 0, 0, tiled=True)  6.01 us
    all_to_all x1, starting transfers between devices, shards(): rows = lax.all_to_all(rows, near, 0, 0, tiled=True).reshape(256, 512)  3.41 us
    all_to_all x1, waiting for transfers between devices, shards(): rows = lax.all_to_all(rows, near, 0, 0, tiled=True).reshape(256, 512)  2.98 us
  transfers between devices with their start and end apart: 13, of which 2 were waited for; matrix products, arithmetic and copies ran while one was open for 1% of the time, Pallas kernels for 17%

profile of v2, /device:TPU:4, one launch (start us, length us, event | category | flops | bytes accessed | tf_op | source)
XLA Modules:
  0.0 83.3 jit_solution(13887813192985539508)
XLA Ops:
  0.6 0.0 copy-start.1
  0.6 0.0 copy-start
  0.7 0.0 copy-start.2
  0.7 0.0 copy-start.7
  0.7 0.0 copy-start.8
  0.7 2.5 %pack.1 = bf16[192,2560]{1,0:T(8,128)(2,1)} custom-call(bf16[192,4096]{1,0:T(8,128)(2,1)} %acts.5, bf16[192,512]{1,0:T(8,128)(2,1)} %cot.7), custom_call_target="tpu_custom_call" | custom-call | bytes 262144 | tf_op jit(solution)/shard_map/pack/pallas_call | solution.py:44
  3.1 1.9 %collective-permute-start = (bf16[192,2560]{1,0:T(8,128)(2,1)}, bf16[192,2560]{1,0:T(8,128)(2,1)S(1)}, u32[]{:S(2)}, u32[]{:S(2)}) collective-permute-start(bf16[192,2560]{1,0:T(8,128)(2,1)} %pack.1), channel_id=1, source_target_pairs={{0,1},{1,0},{2,3},{3,2},{4,5},{5,4},{6,7},{7,6},{8,9},{9,8},{10,11... | collective-permute-start | bytes 2949128 | tf_op jit(solution)/shard_map/ppermute | solution.py:30
  5.1 0.0 copy-done.2
  5.1 5.1 %collective-permute-start.1 = (bf16[256,512]{1,0:T(8,128)(2,1)S(1)}, bf16[256,512]{1,0:T(8,128)(2,1)S(1)}, u32[]{:S(2)}, u32[]{:S(2)}) collective-permute-start(bf16[256,512]{1,0:T(8,128)(2,1)S(1)} %bitcast.4), channel_id=1, source_target_pairs={{0,2},{2,0},{1,3},{3,1},{4,6},{6,4},{5,7},{7,5},{8,10},{10,8},{9,1... | collective-permute-start | bytes 786440 | tf_op jit(solution)/shard_map/ppermute | solution.py:30
  10.2 0.0 copy-done.7
  10.2 0.0 copy-done.8
  10.2 0.7 fold_outer_state.1
  11.0 6.0 %all-to-all-start = ((bf16[8,32,512]{2,1,0:T(8,128)(2,1)}), bf16[8,32,512]{2,1,0:T(8,128)(2,1)}, u32[]{:S(2)}, u32[]{:S(2)}) async-start(bf16[8,32,512]{2,1,0:T(8,128)(2,1)} %bitcast.2), calls=%async_computation | async-start | bytes 524288 | tf_op jit(solution)/shard_map/all_to_all | solution.py:195
  17.0 0.2 collective-permute-done.1.rest_0_
  17.2 0.0 copy-start.5
  17.2 0.0 collective-permute-done.other
  17.2 0.0 copy-done.1
  17.2 0.0 copy-done
  17.2 1.7 %sent_terms.1 = bf16[4,256,512]{2,1,0:T(8,128)(2,1)} custom-call(bf16[192,4096]{1,0:T(8,128)(2,1)S(1)} %copy-done, bf16[192,512]{1,0:T(8,128)(2,1)S(1)} %copy-done.1, bf16[192,2560]{1,0:T(8,128)(2,1)S(1)} %collective-permute-done.other, bf16[256,512]{1,0:T(8,128)(2,1)S(1)} %collective-permute-done.1.rest_0_), custom_call_target="tpu_custom_call" | custom-call | flops 2000000000 | bytes 262144 | tf_op jit(solution)/shard_map/sent_terms/pallas_call | solution.py:44
  18.9 0.0 copy-done.5
  18.9 5.1 %collective-permute-start.5 = (bf16[4,256,512]{2,1,0:T(8,128)(2,1)}, bf16[4,256,512]{2,1,0:T(8,128)(2,1)}, u32[]{:S(2)}, u32[]{:S(2)}) collective-permute-start(bf16[4,256,512]{2,1,0:T(8,128)(2,1)} %sent_terms.1), channel_id=1, source_target_pairs={{0,2},{2,0},{1,3},{3,1},{4,6},{6,4},{5,7},{7,5},{8,10},{10,8},{9,1... | collective-permute-start | bytes 3145736 | tf_op jit(solution)/shard_map/ppermute | solution.py:30
  24.0 1.0 %pad_maximum_fusion.refs_0_ = bf16[2,256,512]{2,1,0:T(8,128)(2,1)S(1)} fusion(bf16[1,256,512]{2,1,0:T(8,128)(2,1)} %bitcast.6, bf16[1,256,512]{2,1,0:T(8,128)(2,1)S(1)} %copy-done.2), kind=kLoop, calls=%fused_computation | loop fusion | flops 262144 | bytes 1048576 | tf_op jit(solution)/shard_map/stack | solution.py:204
  25.1 3.1 %collective-permute-start.2 = (bf16[2,256,512]{2,1,0:T(8,128)(2,1)S(1)}, bf16[2,256,512]{2,1,0:T(8,128)(2,1)}, u32[]{:S(2)}, u32[]{:S(2)}) collective-permute-start(bf16[2,256,512]{2,1,0:T(8,128)(2,1)S(1)} %pad_maximum_fusion.refs_0_), channel_id=1, source_target_pairs={{0,4},{4,8},{8,12},{12,0},{1,5},{5,9},{9,13},{13,1},{2,6},{6,10},{... | collective-permute-start | bytes 1572872 | tf_op jit(solution)/shard_map/ppermute | solution.py:30
  28.2 3.9 %collective-permute-start.3 = (bf16[2,256,512]{2,1,0:T(8,128)(2,1)S(1)}, bf16[2,256,512]{2,1,0:T(8,128)(2,1)}, u32[]{:S(2)}, u32[]{:S(2)}) collective-permute-start(bf16[2,256,512]{2,1,0:T(8,128)(2,1)S(1)} %pad_maximum_fusion.refs_0_), channel_id=1, source_target_pairs={{0,8},{4,12},{8,0},{12,4},{1,9},{5,13},{9,1},{13,5},{2,10},{6,14},... | collective-permute-start | bytes 1572872 | tf_op jit(solution)/shard_map/ppermute | solution.py:30
  32.1 4.5 %collective-permute-start.4 = (bf16[2,256,512]{2,1,0:T(8,128)(2,1)S(1)}, bf16[2,256,512]{2,1,0:T(8,128)(2,1)}, u32[]{:S(2)}, u32[]{:S(2)}) collective-permute-start(bf16[2,256,512]{2,1,0:T(8,128)(2,1)S(1)} %pad_maximum_fusion.refs_0_), channel_id=1, source_target_pairs={{0,12},{4,0},{8,4},{12,8},{1,13},{5,1},{9,5},{13,9},{2,14},{6,2},{... | collective-permute-start | bytes 1572872 | tf_op jit(solution)/shard_map/ppermute | solution.py:30
  36.6 0.0 all-to-all-done.parts
  36.6 1.0 %near_sum.1 = bf16[4,32,512]{2,1,0:T(8,128)(2,1)S(1)} custom-call(bf16[8,32,512]{2,1,0:T(8,128)(2,1)} %all-to-all-done.parts), custom_call_target="tpu_custom_call" | custom-call | flops 1000000000 | bytes 262144 | tf_op jit(solution)/shard_map/near_sum/pallas_call | solution.py:44
  37.6 0.0 copy-start.6
  37.6 0.6 copy-done.6
  38.3 12.8 %all-to-all-start.1 = ((bf16[4,32,512]{2,1,0:T(8,128)(2,1)}), bf16[4,32,512]{2,1,0:T(8,128)(2,1)}, u32[]{:S(2)}, u32[]{:S(2)}) async-start(bf16[4,32,512]{2,1,0:T(8,128)(2,1)} %copy-done.6), calls=%async_computation.1 | async-start | bytes 262144 | tf_op jit(solution)/shard_map/all_to_all | solution.py:209
  51.0 0.0 collective-permute-done.5.came
  51.0 2.7 %kept_terms.1 = (bf16[256,512]{1,0:T(8,128)(2,1)S(1)}, bf16[256,512]{1,0:T(8,128)(2,1)}, bf16[256,512]{1,0:T(8,128)(2,1)}, bf16[256,512]{1,0:T(8,128)(2,1)}) custom-call(bf16[192,4096]{1,0:T(8,128)(2,1)S(1)} %copy-done, bf16[192,512]{1,0:T(8,128)(2,1)S(1)} %copy-done.1, bf16[192,2560]{1,0:T(8,128)(2,1)S(1)} %collective-permute-done.other, ...), custom_call_target="tpu_custom_call" | custom-call | flops 1000000000 | bytes 262144 | tf_op jit(solution)/shard_map/kept_terms/pallas_call | solution.py:44
  53.7 2.9 %collective-permute-start.7 = (bf16[256,512]{1,0:T(8,128)(2,1)}, bf16[256,512]{1,0:T(8,128)(2,1)}, u32[]{:S(2)}, u32[]{:S(2)}) collective-permute-start(bf16[256,512]{1,0:T(8,128)(2,1)} %get-tuple-element.21), channel_id=1, source_target_pairs={{0,4},{4,8},{8,12},{12,0},{1,5},{5,9},{9,13},{13,1},{2,6},{6,10},{... | collective-permute-start | bytes 786440 | tf_op jit(solution)/shard_map/ppermute | solution.py:30
  56.6 3.1 %collective-permute-start.8 = (bf16[256,512]{1,0:T(8,128)(2,1)}, bf16[256,512]{1,0:T(8,128)(2,1)}, u32[]{:S(2)}, u32[]{:S(2)}) collective-permute-start(bf16[256,512]{1,0:T(8,128)(2,1)} %get-tuple-element.22), channel_id=1, source_target_pairs={{0,12},{4,0},{8,4},{12,8},{1,13},{5,1},{9,5},{13,9},{2,14},{6,2},{... | collective-permute-start | bytes 786440 | tf_op jit(solution)/shard_map/ppermute | solution.py:30
  59.7 0.0 collective-permute-done.2.refs_1_
  59.7 6.0 %collective-permute-start.9 = (bf16[256,512]{1,0:T(8,128)(2,1)}, bf16[256,512]{1,0:T(8,128)(2,1)}, u32[]{:S(2)}, u32[]{:S(2)}) collective-permute-start(bf16[256,512]{1,0:T(8,128)(2,1)} %get-tuple-element.23), channel_id=1, source_target_pairs={{0,8},{4,12},{8,0},{12,4},{1,9},{5,13},{9,1},{13,5},{2,10},{6,14},... | collective-permute-start | bytes 786440 | tf_op jit(solution)/shard_map/ppermute | solution.py:30
  65.7 0.0 collective-permute-done.3.refs_2_
  65.8 0.0 collective-permute-done.4.refs_3_
  65.8 2.4 %input_grad_columns.1 = (bf16[192,2048]{1,0:T(8,128)(2,1)S(1)}, bf16[192,2048]{1,0:T(8,128)(2,1)S(1)}) custom-call(bf16[192,512]{1,0:T(8,128)(2,1)S(1)} %copy-done.1, bf16[192,2560]{1,0:T(8,128)(2,1)S(1)} %collective-permute-done.other, bf16[2,256,512]{2,1,0:T(8,128)(2,1)S(1)} %pad_maximum_fusion.refs_0_, ...), custom_call_target="tpu_custom_call" | custom-call | bytes 262144 | tf_op jit(solution)/shard_map/input_grad_columns/pallas_call | solution.py:44
  68.2 0.0 copy-start.3
  68.2 0.7 copy-done.3
  68.9 0.0 copy-start.10
  68.9 0.0 copy-start.11
  68.9 0.0 all-to-all-done.1.parts
  68.9 0.0 copy-start.4
  68.9 1.7 %far_sum.1 = bf16[8,32,512]{2,1,0:T(8,128)(2,1)} custom-call(bf16[4,32,512]{2,1,0:T(8,128)(2,1)} %all-to-all-done.1.parts, bf16[192,2048]{1,0:T(8,128)(2,1)S(1)} %get-tuple-element.20.rest_0_), custom_call_target="tpu_custom_call" | custom-call | bytes 262144 | tf_op jit(solution)/shard_map/far_sum/pallas_call | solution.py:44
  70.6 3.4 %all-to-all-start.2 = ((bf16[8,32,512]{2,1,0:T(8,128)(2,1)}), bf16[8,32,512]{2,1,0:T(8,128)(2,1)S(1)}, u32[]{:S(2)}, u32[]{:S(2)}) async-start(bf16[8,32,512]{2,1,0:T(8,128)(2,1)} %far_sum.1), calls=%async_computation.2 | async-start | bytes 524288 | tf_op jit(solution)/shard_map/all_to_all | solution.py:224
  74.0 1.9 %collective-permute-start.6 = (bf16[192,2048]{1,0:T(8,128)(2,1)S(1)}, bf16[192,2048]{1,0:T(8,128)(2,1)S(1)}, u32[]{:S(2)}, u32[]{:S(2)}) collective-permute-start(bf16[192,2048]{1,0:T(8,128)(2,1)S(1)} %get-tuple-element.20.rest_0_), channel_id=1, source_target_pairs={{0,1},{1,0},{2,3},{3,2},{4,5},{5,4},{6,7},{7,6},{8,9},{9,8},{10,11... | collective-permute-start | bytes 2359304 | tf_op jit(solution)/shard_map/ppermute | solution.py:30
  76.0 0.0 collective-permute-done.7.t1
  76.0 0.0 collective-permute-done.8.t2
  76.0 0.0 collective-permute-done.9.t3
  76.0 0.0 copy-done.10
  76.0 0.0 copy-done.11
  76.0 0.0 copy-done.4
  76.0 2.2 %adam.1 = (f32[256,512]{1,0:T(8,128)S(1)}, bf16[1,256,512]{2,1,0:T(8,128)(2,1)}, bf16[1,256,512]{2,1,0:T(8,128)(2,1)}) custom-call(bf16[256,512]{1,0:T(8,128)(2,1)S(1)} %copy-done.4, bf16[256,512]{1,0:T(8,128)(2,1)} %collective-permute-done.7.t1, bf16[256,512]{1,0:T(8,128)(2,1)} %collective-permute-done.8.t2, bf16[256,512]{1,0:T(8,128)(2,1)} %collective-permute-done.9.t3, ...), custom_call_target="tpu_custom_call" | custom-call | flops 8000000000 | bytes 262144 | tf_op jit(solution)/shard_map/adam/pallas_call | solution.py:44
  78.2 0.0 collective-permute-done.6.mate
  78.2 0.0 copy-start.9
  78.2 1.3 %input_grad.1 = bf16[192,4096]{1,0:T(8,128)(2,1)} custom-call(bf16[192,2048]{1,0:T(8,128)(2,1)S(1)} %get-tuple-element.19.own, bf16[192,2048]{1,0:T(8,128)(2,1)S(1)} %collective-permute-done.6.mate), custom_call_target="tpu_custom_call" | custom-call | flops 500000000 | bytes 262144 | tf_op jit(solution)/shard_map/input_grad/pallas_call | solution.py:44
  79.6 3.0 %all-to-all-done.2 = bf16[8,32,512]{2,1,0:T(8,128)(2,1)S(1)} async-done(((bf16[8,32,512]{2,1,0:T(8,128)(2,1)}), bf16[8,32,512]{2,1,0:T(8,128)(2,1)S(1)}, u32[]{:S(2)}, u32[]{:S(2)}) %all-to-all-start.2) | async-done | bytes 262176 | tf_op jit(solution)/shard_map/all_to_all | solution.py:224
  82.5 0.0 copy-done.9
  82.5 0.8 mix.1
Async XLA Ops:
  0.6 16.6 %copy-start.1 = (bf16[192,512]{1,0:T(8,128)(2,1)S(1)}, bf16[192,512]{1,0:T(8,128)(2,1)}, u32[]{:S(2)}) copy-start(bf16[192,512]{1,0:T(8,128)(2,1)} %cot.7) | copy-start | bytes 589828
  0.6 16.6 %copy-start = (bf16[192,4096]{1,0:T(8,128)(2,1)S(1)}, bf16[192,4096]{1,0:T(8,128)(2,1)}, u32[]{:S(2)}) copy-start(bf16[192,4096]{1,0:T(8,128)(2,1)} %acts.5) | copy-start | bytes 4718596
  0.7 4.4 %copy-start.2 = (bf16[1,256,512]{2,1,0:T(8,128)(2,1)S(1)}, bf16[1,256,512]{2,1,0:T(8,128)(2,1)}, u32[]{:S(2)}) copy-start(bf16[1,256,512]{2,1,0:T(8,128)(2,1)} %weight.3) | copy-start | bytes 786436
  0.7 9.5 %copy-start.7 = (f32[1,1,8,512]{3,2,1,0:T(8,128)S(1)}, f32[1,1,8,512]{3,2,1,0:T(8,128)}, u32[]{:S(2)}) copy-start(f32[1,1,8,512]{3,2,1,0:T(8,128)} %globe.3) | copy-start | bytes 49156
  0.7 9.5 %copy-start.8 = (f32[1,1,8,512]{3,2,1,0:T(8,128)S(1)}, f32[1,1,8,512]{3,2,1,0:T(8,128)}, u32[]{:S(2)}) copy-start(f32[1,1,8,512]{3,2,1,0:T(8,128)} %momentum.3) | copy-start | bytes 49156
  3.1 14.1 %collective-permute-start = (bf16[192,2560]{1,0:T(8,128)(2,1)}, bf16[192,2560]{1,0:T(8,128)(2,1)S(1)}, u32[]{:S(2)}, u32[]{:S(2)}) collective-permute-start(bf16[192,2560]{1,0:T(8,128)(2,1)} %pack.1), channel_id=1, source_target_pairs={{0,1},{1,0},{2,3},{3,2},{4,5},{5,4},{6,7},{7,6},{8,9},{9,8},{10,11... | collective-permute-start | bytes 2949128 | tf_op jit(solution)/shard_map/ppermute | solution.py:30
  5.1 12.1 %collective-permute-start.1 = (bf16[256,512]{1,0:T(8,128)(2,1)S(1)}, bf16[256,512]{1,0:T(8,128)(2,1)S(1)}, u32[]{:S(2)}, u32[]{:S(2)}) collective-permute-start(bf16[256,512]{1,0:T(8,128)(2,1)S(1)} %bitcast.4), channel_id=1, source_target_pairs={{0,2},{2,0},{1,3},{3,1},{4,6},{6,4},{5,7},{7,5},{8,10},{10,8},{9,1... | collective-permute-start | bytes 786440 | tf_op jit(solution)/shard_map/ppermute | solution.py:30
  11.0 25.7 %all-to-all-start = ((bf16[8,32,512]{2,1,0:T(8,128)(2,1)}), bf16[8,32,512]{2,1,0:T(8,128)(2,1)}, u32[]{:S(2)}, u32[]{:S(2)}) async-start(bf16[8,32,512]{2,1,0:T(8,128)(2,1)} %bitcast.2), calls=%async_computation | async-start | bytes 524288 | tf_op jit(solution)/shard_map/all_to_all | solution.py:195
  17.2 1.8 %copy-start.5 = (bf16[256,512]{1,0:T(8,128)(2,1)}, bf16[256,512]{1,0:T(8,128)(2,1)S(1)}, u32[]{:S(2)}) copy-start(bf16[256,512]{1,0:T(8,128)(2,1)S(1)} %collective-permute-done.1.rest_0_) | copy-start | bytes 786436
  18.9 32.1 %collective-permute-start.5 = (bf16[4,256,512]{2,1,0:T(8,128)(2,1)}, bf16[4,256,512]{2,1,0:T(8,128)(2,1)}, u32[]{:S(2)}, u32[]{:S(2)}) collective-permute-start(bf16[4,256,512]{2,1,0:T(8,128)(2,1)} %sent_terms.1), channel_id=1, source_target_pairs={{0,2},{2,0},{1,3},{3,1},{4,6},{6,4},{5,7},{7,5},{8,10},{10,8},{9,1... | collective-permute-start | bytes 3145736 | tf_op jit(solution)/shard_map/ppermute | solution.py:30
  25.1 34.7 %collective-permute-start.2 = (bf16[2,256,512]{2,1,0:T(8,128)(2,1)S(1)}, bf16[2,256,512]{2,1,0:T(8,128)(2,1)}, u32[]{:S(2)}, u32[]{:S(2)}) collective-permute-start(bf16[2,256,512]{2,1,0:T(8,128)(2,1)S(1)} %pad_maximum_fusion.refs_0_), channel_id=1, source_target_pairs={{0,4},{4,8},{8,12},{12,0},{1,5},{5,9},{9,13},{13,1},{2,6},{6,10},{... | collective-permute-start | bytes 1572872 | tf_op jit(solution)/shard_map/ppermute | solution.py:30
  28.2 37.6 %collective-permute-start.3 = (bf16[2,256,512]{2,1,0:T(8,128)(2,1)S(1)}, bf16[2,256,512]{2,1,0:T(8,128)(2,1)}, u32[]{:S(2)}, u32[]{:S(2)}) collective-permute-start(bf16[2,256,512]{2,1,0:T(8,128)(2,1)S(1)} %pad_maximum_fusion.refs_0_), channel_id=1, source_target_pairs={{0,8},{4,12},{8,0},{12,4},{1,9},{5,13},{9,1},{13,5},{2,10},{6,14},... | collective-permute-start | bytes 1572872 | tf_op jit(solution)/shard_map/ppermute | solution.py:30
  32.1 33.7 %collective-permute-start.4 = (bf16[2,256,512]{2,1,0:T(8,128)(2,1)S(1)}, bf16[2,256,512]{2,1,0:T(8,128)(2,1)}, u32[]{:S(2)}, u32[]{:S(2)}) collective-permute-start(bf16[2,256,512]{2,1,0:T(8,128)(2,1)S(1)} %pad_maximum_fusion.refs_0_), channel_id=1, source_target_pairs={{0,12},{4,0},{8,4},{12,8},{1,13},{5,1},{9,5},{13,9},{2,14},{6,2},{... | collective-permute-start | bytes 1572872 | tf_op jit(solution)/shard_map/ppermute | solution.py:30
  37.6 0.6 copy-start.6
  38.3 30.6 %all-to-all-start.1 = ((bf16[4,32,512]{2,1,0:T(8,128)(2,1)}), bf16[4,32,512]{2,1,0:T(8,128)(2,1)}, u32[]{:S(2)}, u32[]{:S(2)}) async-start(bf16[4,32,512]{2,1,0:T(8,128)(2,1)} %copy-done.6), calls=%async_computation.1 | async-start | bytes 262144 | tf_op jit(solution)/shard_map/all_to_all | solution.py:209
  53.7 22.2 %collective-permute-start.7 = (bf16[256,512]{1,0:T(8,128)(2,1)}, bf16[256,512]{1,0:T(8,128)(2,1)}, u32[]{:S(2)}, u32[]{:S(2)}) collective-permute-start(bf16[256,512]{1,0:T(8,128)(2,1)} %get-tuple-element.21), channel_id=1, source_target_pairs={{0,4},{4,8},{8,12},{12,0},{1,5},{5,9},{9,13},{13,1},{2,6},{6,10},{... | collective-permute-start | bytes 786440 | tf_op jit(solution)/shard_map/ppermute | solution.py:30
  56.6 19.4 %collective-permute-start.8 = (bf16[256,512]{1,0:T(8,128)(2,1)}, bf16[256,512]{1,0:T(8,128)(2,1)}, u32[]{:S(2)}, u32[]{:S(2)}) collective-permute-start(bf16[256,512]{1,0:T(8,128)(2,1)} %get-tuple-element.22), channel_id=1, source_target_pairs={{0,12},{4,0},{8,4},{12,8},{1,13},{5,1},{9,5},{13,9},{2,14},{6,2},{... | collective-permute-start | bytes 786440 | tf_op jit(solution)/shard_map/ppermute | solution.py:30
  59.7 16.3 %collective-permute-start.9 = (bf16[256,512]{1,0:T(8,128)(2,1)}, bf16[256,512]{1,0:T(8,128)(2,1)}, u32[]{:S(2)}, u32[]{:S(2)}) collective-permute-start(bf16[256,512]{1,0:T(8,128)(2,1)} %get-tuple-element.23), channel_id=1, source_target_pairs={{0,8},{4,12},{8,0},{12,4},{1,9},{5,13},{9,1},{13,5},{2,10},{6,14},... | collective-permute-start | bytes 786440 | tf_op jit(solution)/shard_map/ppermute | solution.py:30
  68.2 0.7 copy-start.3
  68.9 7.1 %copy-start.10 = (bf16[1,256,512]{2,1,0:T(8,128)(2,1)S(1)}, bf16[1,256,512]{2,1,0:T(8,128)(2,1)}, u32[]{:S(2)}) copy-start(bf16[1,256,512]{2,1,0:T(8,128)(2,1)} %adam_first.1) | copy-start | bytes 786436
  68.9 7.1 %copy-start.11 = (bf16[1,256,512]{2,1,0:T(8,128)(2,1)S(1)}, bf16[1,256,512]{2,1,0:T(8,128)(2,1)}, u32[]{:S(2)}) copy-start(bf16[1,256,512]{2,1,0:T(8,128)(2,1)} %adam_second.1) | copy-start | bytes 786436
  68.9 7.1 %copy-start.4 = (bf16[256,512]{1,0:T(8,128)(2,1)S(1)}, bf16[256,512]{1,0:T(8,128)(2,1)}, u32[]{:S(2)}) copy-start(bf16[256,512]{1,0:T(8,128)(2,1)} %copy-done.3) | copy-start | bytes 786436
  70.6 11.9 %all-to-all-start.2 = ((bf16[8,32,512]{2,1,0:T(8,128)(2,1)}), bf16[8,32,512]{2,1,0:T(8,128)(2,1)S(1)}, u32[]{:S(2)}, u32[]{:S(2)}) async-start(bf16[8,32,512]{2,1,0:T(8,128)(2,1)} %far_sum.1), calls=%async_computation.2 | async-start | bytes 524288 | tf_op jit(solution)/shard_map/all_to_all | solution.py:224
  74.0 4.2 %collective-permute-start.6 = (bf16[192,2048]{1,0:T(8,128)(2,1)S(1)}, bf16[192,2048]{1,0:T(8,128)(2,1)S(1)}, u32[]{:S(2)}, u32[]{:S(2)}) collective-permute-start(bf16[192,2048]{1,0:T(8,128)(2,1)S(1)} %get-tuple-element.20.rest_0_), channel_id=1, source_target_pairs={{0,1},{1,0},{2,3},{3,2},{4,5},{5,4},{6,7},{7,6},{8,9},{9,8},{10,11... | collective-permute-start | bytes 2359304 | tf_op jit(solution)/shard_map/ppermute | solution.py:30
  78.2 4.3 %copy-start.9 = (f32[1,1,8,512]{3,2,1,0:T(8,128)S(1)}, f32[1,1,8,512]{3,2,1,0:T(8,128)}, u32[]{:S(2)}) copy-start(f32[1,1,8,512]{3,2,1,0:T(8,128)} %momentum.3) | copy-start | bytes 49156

commit v3 on v2

--- a/solution.py
+++ b/solution.py
@@ -178,7 +178,7 @@
         pack_kernel,
         (acts, cot),
         shaped(tokens, 2560),
-        "pack", limit=60,
+        "pack", weight=500000000, limit=60,
         loose=2,
         scratch=[pltpu.SemaphoreType.DMA((9,))],
         space=pltpu.HBM,
@@ -194,7 +194,7 @@
     near = ("ylo", "zlo")
     parts = lax.all_to_all(blocks.reshape(8, 32, 512), near, 0, 0, tiled=True)
     send = call(
-        sent_kernel, (acts, cot, other, across), shaped(4, 256, 512), "sent_terms", weight=2000000000, loose=1
+        sent_kernel, (acts, cot, other, blocks, across), shaped(4, 256, 512), "sent_terms", weight=500000000, loose=2
     )
     came = permute(send, "yhi", 2, 1)
 
@@ -205,18 +205,18 @@
     pairs = [pair] + [permute(pair, "x", 4, s) for s in (1, 3, 2)]
     pairs = [pairs[0], pairs[1], pairs[3], pairs[2]]
 
-    parts = call(functools.partial(spread_kernel, 1.0), (parts,), shaped(4, 32, 512), "near_sum", weight=1000000000)
+    parts = call(functools.partial(spread_kernel, 1.0), (parts,), shaped(4, 32, 512), "near_sum")
     parts = lax.all_to_all(parts, "zhi", 0, 0, tiled=True)
     mine, sent = call(
         input_kernel,
-        (cot, other, *pairs, keep[0]),
+        (cot, other, *pairs, parts, keep[1]),
         [shaped(tokens, 2048)] * 2,
         "input_grad_columns",
-        loose=1,
+        loose=2,
     )
     rows = call(
         functools.partial(spread_kernel, SCALE),
-        (parts, sent),
+        (parts, keep[1]),
         shaped(8, 32, 512),
         "far_sum",
         loose=1,
@@ -225,7 +225,7 @@
 
     mate = permute(sent, "core", 2, 1)
     input_grad = call(
-        join_kernel, (mine, mate), shaped(tokens, 4096), "input_grad", weight=500000000, loose=0
+        join_kernel, (mine, mate), shaped(tokens, 4096), "input_grad", loose=0
     )
 
     half, new_first, new_second = call(
@@ -239,7 +239,7 @@
         mix_kernel,
         (half, rows, global_weight, outer_momentum),
         [shaped(1, 256, 512), outer, outer],
-        "mix", weight=500000000,
+        "mix", weight=4000000000,
     )
     return input_grad, new_weight, new_first, new_second, new_global, new_momentum
 

time: 84.2 us -> 82.7 us (0.982)
  the two profiles are of different devices: /device:TPU:4 before, /device:TPU:1 now
where the time goes in v3:
time: 82.7 us; the launch traced here: 81.8 us
  starting transfers between devices  55.6 us (67%)
  Pallas kernels  16.1 us (19%)
  waiting for transfers between devices  6.76 us (8%)
  local copies, waits for them, and re-layouts  1.41 us (2%)
  other arithmetic  1 us (1%)
  between operations  0.99 us (1%)
    ppermute x10, starting transfers between devices, permute(): lax.ppermute(array, axis, [(i, (i + shift) % size) for i in range(size)])  33.8 us
    pallas_call x10, Pallas kernels, call(): pl.pallas_call(kernel, in_specs=[pl.BlockSpec(memory_space=pltpu.VMEM)] *...  16.1 us
    all_to_all x1, starting transfers between devices, shards(): parts = lax.all_to_all(parts, 'zhi', 0, 0, tiled=True)  14.3 us
    ppermute x10, waiting for transfers between devices, permute(): lax.ppermute(array, axis, [(i, (i + shift) % size) for i in range(size)])  6.76 us
    all_to_all x1, starting transfers between devices, shards(): rows = lax.all_to_all(rows, near, 0, 0, tiled=True).reshape(256, 512)  4.04 us
    all_to_all x1, starting transfers between devices, shards(): parts = lax.all_to_all(blocks.reshape(8, 32, 512), near, 0, 0, tiled=True)  3.41 us
  transfers between devices with their start and end apart: 13, of which 2 were waited for; matrix products, arithmetic and copies ran while one was open for 1% of the time, Pallas kernels for 15%

profile of v3, /device:TPU:1, one launch (start us, length us, event | category | flops | bytes accessed | tf_op | source)
XLA Modules:
  0.0 81.8 jit_solution(14325657636942164862)
XLA Ops:
  0.6 0.0 copy-start.1
  0.6 0.0 copy-start
  0.7 0.0 copy-start.3
  0.7 0.0 copy-start.8
  0.7 0.0 copy-start.7
  0.7 2.5 %pack.1 = bf16[192,2560]{1,0:T(8,128)(2,1)} custom-call(bf16[192,4096]{1,0:T(8,128)(2,1)} %acts.5, bf16[192,512]{1,0:T(8,128)(2,1)} %cot.7), custom_call_target="tpu_custom_call" | custom-call | flops 500000000 | bytes 262144 | tf_op jit(solution)/shard_map/pack/pallas_call | solution.py:44
  3.1 8.8 %collective-permute-start = (bf16[192,2560]{1,0:T(8,128)(2,1)}, bf16[192,2560]{1,0:T(8,128)(2,1)S(1)}, u32[]{:S(2)}, u32[]{:S(2)}) collective-permute-start(bf16[192,2560]{1,0:T(8,128)(2,1)} %pack.1), channel_id=1, source_target_pairs={{0,1},{1,0},{2,3},{3,2},{4,5},{5,4},{6,7},{7,6},{8,9},{9,8},{10,11... | collective-permute-start | bytes 2949128 | tf_op jit(solution)/shard_map/ppermute | solution.py:30
  11.9 0.0 copy-done.3
  11.9 1.9 %collective-permute-start.1 = (bf16[256,512]{1,0:T(8,128)(2,1)S(1)}, bf16[256,512]{1,0:T(8,128)(2,1)S(1)}, u32[]{:S(2)}, u32[]{:S(2)}) collective-permute-start(bf16[256,512]{1,0:T(8,128)(2,1)S(1)} %bitcast.5), channel_id=1, source_target_pairs={{0,2},{2,0},{1,3},{3,1},{4,6},{6,4},{5,7},{7,5},{8,10},{10,8},{9,1... | collective-permute-start | bytes 786440 | tf_op jit(solution)/shard_map/ppermute | solution.py:30
  13.9 0.0 copy-done.8
  13.9 0.0 copy-done.7
  13.9 0.7 fold_outer_state.1.rest_0_
  14.6 3.4 %all-to-all-start = ((bf16[8,32,512]{2,1,0:T(8,128)(2,1)}), bf16[8,32,512]{2,1,0:T(8,128)(2,1)S(1)}, u32[]{:S(2)}, u32[]{:S(2)}) async-start(bf16[8,32,512]{2,1,0:T(8,128)(2,1)} %bitcast.2), calls=%async_computation | async-start | bytes 524288 | tf_op jit(solution)/shard_map/all_to_all | solution.py:195
  18.1 0.0 copy-start.4
  18.1 5.2 %collective-permute-done.1.rest_1_ = bf16[256,512]{1,0:T(8,128)(2,1)S(1)} collective-permute-done((bf16[256,512]{1,0:T(8,128)(2,1)S(1)}, bf16[256,512]{1,0:T(8,128)(2,1)S(1)}, u32[]{:S(2)}, u32[]{:S(2)}) %collective-permute-start.1) | collective-permute-done | bytes 262176 | tf_op jit(solution)/shard_map/ppermute | solution.py:30
  23.3 0.0 copy-start.2
  23.3 0.0 collective-permute-done.other
  23.3 0.0 copy-done.1
  23.3 0.0 copy-done
  23.3 1.7 %sent_terms.1 = bf16[4,256,512]{2,1,0:T(8,128)(2,1)} custom-call(bf16[192,4096]{1,0:T(8,128)(2,1)S(1)} %copy-done, bf16[192,512]{1,0:T(8,128)(2,1)S(1)} %copy-done.1, bf16[192,2560]{1,0:T(8,128)(2,1)S(1)} %collective-permute-done.other, bf16[256,512]{1,0:T(8,128)(2,1)} %fold_outer_state.1.rest_0_, bf16[256,512]{1,0:T(8,128)(2,1)S(1)} %collective-permute-done.1.rest_1_), custom_call_target="tpu_custom_call" | custom-call | flops 500000000 | bytes 262144 | tf_op jit(solution)/shard_map/sent_terms/pallas_call | solution.py:44
  25.0 0.0 copy-done.2
  25.0 2.1 %collective-permute-start.5 = (bf16[4,256,512]{2,1,0:T(8,128)(2,1)}, bf16[4,256,512]{2,1,0:T(8,128)(2,1)}, u32[]{:S(2)}, u32[]{:S(2)}) collective-permute-start(bf16[4,256,512]{2,1,0:T(8,128)(2,1)} %sent_terms.1), channel_id=1, source_target_pairs={{0,2},{2,0},{1,3},{3,1},{4,6},{6,4},{5,7},{7,5},{8,10},{10,8},{9,1... | collective-permute-start | bytes 3145736 | tf_op jit(solution)/shard_map/ppermute | solution.py:30
  27.2 0.0 copy-done.4
  27.2 1.0 %pad_maximum_fusion.refs_0_ = bf16[2,256,512]{2,1,0:T(8,128)(2,1)S(1)} fusion(bf16[1,256,512]{2,1,0:T(8,128)(2,1)} %bitcast.4, bf16[1,256,512]{2,1,0:T(8,128)(2,1)S(1)} %copy-done.4), kind=kLoop, calls=%fused_computation | loop fusion | flops 262144 | bytes 1048576 | tf_op jit(solution)/shard_map/stack | solution.py:204
  28.2 1.9 %collective-permute-start.4 = (bf16[2,256,512]{2,1,0:T(8,128)(2,1)S(1)}, bf16[2,256,512]{2,1,0:T(8,128)(2,1)}, u32[]{:S(2)}, u32[]{:S(2)}) collective-permute-start(bf16[2,256,512]{2,1,0:T(8,128)(2,1)S(1)} %pad_maximum_fusion.refs_0_), channel_id=1, source_target_pairs={{0,12},{4,0},{8,4},{12,8},{1,13},{5,1},{9,5},{13,9},{2,14},{6,2},{... | collective-permute-start | bytes 1572872 | tf_op jit(solution)/shard_map/ppermute | solution.py:30
  30.1 2.2 %collective-permute-start.3 = (bf16[2,256,512]{2,1,0:T(8,128)(2,1)S(1)}, bf16[2,256,512]{2,1,0:T(8,128)(2,1)}, u32[]{:S(2)}, u32[]{:S(2)}) collective-permute-start(bf16[2,256,512]{2,1,0:T(8,128)(2,1)S(1)} %pad_maximum_fusion.refs_0_), channel_id=1, source_target_pairs={{0,8},{4,12},{8,0},{12,4},{1,9},{5,13},{9,1},{13,5},{2,10},{6,14},... | collective-permute-start | bytes 1572872 | tf_op jit(solution)/shard_map/ppermute | solution.py:30
  32.3 3.1 %collective-permute-start.2 = (bf16[2,256,512]{2,1,0:T(8,128)(2,1)S(1)}, bf16[2,256,512]{2,1,0:T(8,128)(2,1)}, u32[]{:S(2)}, u32[]{:S(2)}) collective-permute-start(bf16[2,256,512]{2,1,0:T(8,128)(2,1)S(1)} %pad_maximum_fusion.refs_0_), channel_id=1, source_target_pairs={{0,4},{4,8},{8,12},{12,0},{1,5},{5,9},{9,13},{13,1},{2,6},{6,10},{... | collective-permute-start | bytes 1572872 | tf_op jit(solution)/shard_map/ppermute | solution.py:30
  35.4 0.0 all-to-all-done.parts
  35.5 0.0 copy-start.6
  35.5 0.6 copy-done.6
  36.1 14.3 %all-to-all-start.1 = ((bf16[4,32,512]{2,1,0:T(8,128)(2,1)}), bf16[4,32,512]{2,1,0:T(8,128)(2,1)S(1)}, u32[]{:S(2)}, u32[]{:S(2)}) async-start(bf16[4,32,512]{2,1,0:T(8,128)(2,1)} %copy-done.6), calls=%async_computation.1 | async-start | bytes 262144 | tf_op jit(solution)/shard_map/all_to_all | solution.py:209
  50.4 1.5 %collective-permute-done.5.came = bf16[4,256,512]{2,1,0:T(8,128)(2,1)} collective-permute-done((bf16[4,256,512]{2,1,0:T(8,128)(2,1)}, bf16[4,256,512]{2,1,0:T(8,128)(2,1)}, u32[]{:S(2)}, u32[]{:S(2)}) %collective-permute-start.5) | collective-permute-done | bytes 1048608 | tf_op jit(solution)/shard_map/ppermute | solution.py:30
  51.9 2.7 %kept_terms.1 = (bf16[256,512]{1,0:T(8,128)(2,1)S(1)}, bf16[256,512]{1,0:T(8,128)(2,1)}, bf16[256,512]{1,0:T(8,128)(2,1)}, bf16[256,512]{1,0:T(8,128)(2,1)}) custom-call(bf16[192,4096]{1,0:T(8,128)(2,1)S(1)} %copy-done, bf16[192,512]{1,0:T(8,128)(2,1)S(1)} %copy-done.1, bf16[192,2560]{1,0:T(8,128)(2,1)S(1)} %collective-permute-done.other, ...), custom_call_target="tpu_custom_call" | custom-call | flops 1000000000 | bytes 262144 | tf_op jit(solution)/shard_map/kept_terms/pallas_call | solution.py:44
  54.6 0.0 copy-start.12
  54.6 0.7 copy-done.12
  55.3 2.4 %collective-permute-start.8 = (bf16[256,512]{1,0:T(8,128)(2,1)}, bf16[256,512]{1,0:T(8,128)(2,1)}, u32[]{:S(2)}, u32[]{:S(2)}) collective-permute-start(bf16[256,512]{1,0:T(8,128)(2,1)} %get-tuple-element.22), channel_id=1, source_target_pairs={{0,12},{4,0},{8,4},{12,8},{1,13},{5,1},{9,5},{13,9},{2,14},{6,2},{... | collective-permute-start | bytes 786440 | tf_op jit(solution)/shard_map/ppermute | solution.py:30
  57.8 3.1 %collective-permute-start.9 = (bf16[256,512]{1,0:T(8,128)(2,1)}, bf16[256,512]{1,0:T(8,128)(2,1)}, u32[]{:S(2)}, u32[]{:S(2)}) collective-permute-start(bf16[256,512]{1,0:T(8,128)(2,1)} %get-tuple-element.23), channel_id=1, source_target_pairs={{0,8},{4,12},{8,0},{12,4},{1,9},{5,13},{9,1},{13,5},{2,10},{6,14},... | collective-permute-start | bytes 786440 | tf_op jit(solution)/shard_map/ppermute | solution.py:30
  60.9 0.0 collective-permute-done.4.refs_3_
  60.9 1.9 %collective-permute-start.7 = (bf16[256,512]{1,0:T(8,128)(2,1)}, bf16[256,512]{1,0:T(8,128)(2,1)}, u32[]{:S(2)}, u32[]{:S(2)}) collective-permute-start(bf16[256,512]{1,0:T(8,128)(2,1)} %get-tuple-element.18.refs_5_.rest_0_), channel_id=1, source_target_pairs={{0,4},{4,8},{8,12},{12,0},{1,5},{5,9},{9,13},{13,1},{2,6},{6,10},{... | collective-permute-start | bytes 786440 | tf_op jit(solution)/shard_map/ppermute | solution.py:30
  62.8 0.0 all-to-all-done.1.refs_4_.parts
  62.9 0.7 far_sum.1
  63.6 4.0 %all-to-all-start.2 = ((bf16[8,32,512]{2,1,0:T(8,128)(2,1)}), bf16[8,32,512]{2,1,0:T(8,128)(2,1)}, u32[]{:S(2)}, u32[]{:S(2)}) async-start(bf16[8,32,512]{2,1,0:T(8,128)(2,1)} %far_sum.1), calls=%async_computation.2 | async-start | bytes 524288 | tf_op jit(solution)/shard_map/all_to_all | solution.py:224
  67.6 0.0 copy-start.5
  67.6 0.0 copy-start.10
  67.7 0.0 copy-start.11
  67.7 0.0 copy-start.13
  67.7 0.0 collective-permute-done.3.refs_2_
  67.7 0.0 collective-permute-done.2.refs_1_
  67.7 2.5 %input_grad_columns.1 = (bf16[192,2048]{1,0:T(8,128)(2,1)S(1)}, bf16[192,2048]{1,0:T(8,128)(2,1)S(1)}) custom-call(bf16[192,512]{1,0:T(8,128)(2,1)S(1)} %copy-done.1, bf16[192,2560]{1,0:T(8,128)(2,1)S(1)} %collective-permute-done.other, bf16[2,256,512]{2,1,0:T(8,128)(2,1)S(1)} %pad_maximum_fusion.refs_0_, ...), custom_call_target="tpu_custom_call" | custom-call | bytes 262144 | tf_op jit(solution)/shard_map/input_grad_columns/pallas_call | solution.py:44
  70.2 6.3 %collective-permute-start.6 = (bf16[192,2048]{1,0:T(8,128)(2,1)S(1)}, bf16[192,2048]{1,0:T(8,128)(2,1)S(1)}, u32[]{:S(2)}, u32[]{:S(2)}) collective-permute-start(bf16[192,2048]{1,0:T(8,128)(2,1)S(1)} %get-tuple-element.20), channel_id=1, source_target_pairs={{0,1},{1,0},{2,3},{3,2},{4,5},{5,4},{6,7},{7,6},{8,9},{9,8},{10,11... | collective-permute-start | bytes 2359304 | tf_op jit(solution)/shard_map/ppermute | solution.py:30
  76.5 0.0 collective-permute-done.8.t2
  76.5 0.0 collective-permute-done.9.t3
  76.5 0.0 collective-permute-done.7.t1
  76.5 0.0 copy-done.5
  76.5 0.0 copy-done.10
  76.6 0.0 copy-done.11
  76.6 0.0 copy-done.13
  76.6 2.2 %adam.1 = (f32[256,512]{1,0:T(8,128)S(1)}, bf16[1,256,512]{2,1,0:T(8,128)(2,1)}, bf16[1,256,512]{2,1,0:T(8,128)(2,1)}) custom-call(bf16[256,512]{1,0:T(8,128)(2,1)S(1)} %copy-done.13, bf16[256,512]{1,0:T(8,128)(2,1)} %collective-permute-done.7.t1, bf16[256,512]{1,0:T(8,128)(2,1)} %collective-permute-done.8.t2, bf16[256,512]{1,0:T(8,128)(2,1)} %collective-permute-done.9.t3, ...), custom_call_target="tpu_custom_call" | custom-call | flops 8000000000 | bytes 262144 | tf_op jit(solution)/shard_map/adam/pallas_call | solution.py:44
  78.8 0.0 collective-permute-done.6.mate
  78.8 0.0 copy-start.9
  78.8 1.4 %input_grad.1 = bf16[192,4096]{1,0:T(8,128)(2,1)} custom-call(bf16[192,2048]{1,0:T(8,128)(2,1)S(1)} %get-tuple-element.19.own, bf16[192,2048]{1,0:T(8,128)(2,1)S(1)} %collective-permute-done.6.mate), custom_call_target="tpu_custom_call" | custom-call | bytes 262144 | tf_op jit(solution)/shard_map/input_grad/pallas_call | solution.py:44
  80.1 0.0 all-to-all-done.2
  80.1 0.0 copy-done.9
  80.1 1.7 %mix.1 = (bf16[1,256,512]{2,1,0:T(8,128)(2,1)}, f32[1,1,8,512]{3,2,1,0:T(8,128)}, f32[1,1,8,512]{3,2,1,0:T(8,128)}) custom-call(f32[256,512]{1,0:T(8,128)S(1)} %get-tuple-element.24.half, bf16[256,512]{1,0:T(8,128)(2,1)} %bitcast.3.rows, f32[1,1,8,512]{3,2,1,0:T(8,128)S(1)} %copy-done.7, f32[1,1,8,512]{3,2,1,0:T(8,128)S(1)} %copy-done.9), custom_call_target="tpu_custom_call" | custom-call | flops 4000000000 | bytes 262144 | tf_op jit(solution)/shard_map/mix/pallas_call | solution.py:44
  (1 shorter events, 0.0 us)
Async XLA Ops:
  0.6 22.6 %copy-start.1 = (bf16[192,512]{1,0:T(8,128)(2,1)S(1)}, bf16[192,512]{1,0:T(8,128)(2,1)}, u32[]{:S(2)}) copy-start(bf16[192,512]{1,0:T(8,128)(2,1)} %cot.7) | copy-start | bytes 589828
  0.6 22.6 %copy-start = (bf16[192,4096]{1,0:T(8,128)(2,1)S(1)}, bf16[192,4096]{1,0:T(8,128)(2,1)}, u32[]{:S(2)}) copy-start(bf16[192,4096]{1,0:T(8,128)(2,1)} %acts.5) | copy-start | bytes 4718596
  0.7 11.3 %copy-start.3 = (bf16[1,256,512]{2,1,0:T(8,128)(2,1)S(1)}, bf16[1,256,512]{2,1,0:T(8,128)(2,1)}, u32[]{:S(2)}) copy-start(bf16[1,256,512]{2,1,0:T(8,128)(2,1)} %weight.3) | copy-start | bytes 786436
  0.7 13.2 %copy-start.8 = (f32[1,1,8,512]{3,2,1,0:T(8,128)S(1)}, f32[1,1,8,512]{3,2,1,0:T(8,128)}, u32[]{:S(2)}) copy-start(f32[1,1,8,512]{3,2,1,0:T(8,128)} %momentum.3) | copy-start | bytes 49156
  0.7 13.2 %copy-start.7 = (f32[1,1,8,512]{3,2,1,0:T(8,128)S(1)}, f32[1,1,8,512]{3,2,1,0:T(8,128)}, u32[]{:S(2)}) copy-start(f32[1,1,8,512]{3,2,1,0:T(8,128)} %globe.3) | copy-start | bytes 49156
  3.1 20.1 %collective-permute-start = (bf16[192,2560]{1,0:T(8,128)(2,1)}, bf16[192,2560]{1,0:T(8,128)(2,1)S(1)}, u32[]{:S(2)}, u32[]{:S(2)}) collective-permute-start(bf16[192,2560]{1,0:T(8,128)(2,1)} %pack.1), channel_id=1, source_target_pairs={{0,1},{1,0},{2,3},{3,2},{4,5},{5,4},{6,7},{7,6},{8,9},{9,8},{10,11... | collective-permute-start | bytes 2949128 | tf_op jit(solution)/shard_map/ppermute | solution.py:30
  11.9 11.3 %collective-permute-start.1 = (bf16[256,512]{1,0:T(8,128)(2,1)S(1)}, bf16[256,512]{1,0:T(8,128)(2,1)S(1)}, u32[]{:S(2)}, u32[]{:S(2)}) collective-permute-start(bf16[256,512]{1,0:T(8,128)(2,1)S(1)} %bitcast.5), channel_id=1, source_target_pairs={{0,2},{2,0},{1,3},{3,1},{4,6},{6,4},{5,7},{7,5},{8,10},{10,8},{9,1... | collective-permute-start | bytes 786440 | tf_op jit(solution)/shard_map/ppermute | solution.py:30
  14.6 20.8 %all-to-all-start = ((bf16[8,32,512]{2,1,0:T(8,128)(2,1)}), bf16[8,32,512]{2,1,0:T(8,128)(2,1)S(1)}, u32[]{:S(2)}, u32[]{:S(2)}) async-start(bf16[8,32,512]{2,1,0:T(8,128)(2,1)} %bitcast.2), calls=%async_computation | async-start | bytes 524288 | tf_op jit(solution)/shard_map/all_to_all | solution.py:195
  18.1 9.1 %copy-start.4 = (bf16[1,256,512]{2,1,0:T(8,128)(2,1)S(1)}, bf16[1,256,512]{2,1,0:T(8,128)(2,1)}, u32[]{:S(2)}) copy-start(bf16[1,256,512]{2,1,0:T(8,128)(2,1)} %weight.3) | copy-start | bytes 786436
  23.3 1.8 %copy-start.2 = (bf16[256,512]{1,0:T(8,128)(2,1)}, bf16[256,512]{1,0:T(8,128)(2,1)S(1)}, u32[]{:S(2)}) copy-start(bf16[256,512]{1,0:T(8,128)(2,1)S(1)} %collective-permute-done.1.rest_1_) | copy-start | bytes 786436
  25.0 26.9 %collective-permute-start.5 = (bf16[4,256,512]{2,1,0:T(8,128)(2,1)}, bf16[4,256,512]{2,1,0:T(8,128)(2,1)}, u32[]{:S(2)}, u32[]{:S(2)}) collective-permute-start(bf16[4,256,512]{2,1,0:T(8,128)(2,1)} %sent_terms.1), channel_id=1, source_target_pairs={{0,2},{2,0},{1,3},{3,1},{4,6},{6,4},{5,7},{7,5},{8,10},{10,8},{9,1... | collective-permute-start | bytes 3145736 | tf_op jit(solution)/shard_map/ppermute | solution.py:30
  28.2 32.7 %collective-permute-start.4 = (bf16[2,256,512]{2,1,0:T(8,128)(2,1)S(1)}, bf16[2,256,512]{2,1,0:T(8,128)(2,1)}, u32[]{:S(2)}, u32[]{:S(2)}) collective-permute-start(bf16[2,256,512]{2,1,0:T(8,128)(2,1)S(1)} %pad_maximum_fusion.refs_0_), channel_id=1, source_target_pairs={{0,12},{4,0},{8,4},{12,8},{1,13},{5,1},{9,5},{13,9},{2,14},{6,2},{... | collective-permute-start | bytes 1572872 | tf_op jit(solution)/shard_map/ppermute | solution.py:30
  30.1 37.6 %collective-permute-start.3 = (bf16[2,256,512]{2,1,0:T(8,128)(2,1)S(1)}, bf16[2,256,512]{2,1,0:T(8,128)(2,1)}, u32[]{:S(2)}, u32[]{:S(2)}) collective-permute-start(bf16[2,256,512]{2,1,0:T(8,128)(2,1)S(1)} %pad_maximum_fusion.refs_0_), channel_id=1, source_target_pairs={{0,8},{4,12},{8,0},{12,4},{1,9},{5,13},{9,1},{13,5},{2,10},{6,14},... | collective-permute-start | bytes 1572872 | tf_op jit(solution)/shard_map/ppermute | solution.py:30
  32.3 35.4 %collective-permute-start.2 = (bf16[2,256,512]{2,1,0:T(8,128)(2,1)S(1)}, bf16[2,256,512]{2,1,0:T(8,128)(2,1)}, u32[]{:S(2)}, u32[]{:S(2)}) collective-permute-start(bf16[2,256,512]{2,1,0:T(8,128)(2,1)S(1)} %pad_maximum_fusion.refs_0_), channel_id=1, source_target_pairs={{0,4},{4,8},{8,12},{12,0},{1,5},{5,9},{9,13},{13,1},{2,6},{6,10},{... | collective-permute-start | bytes 1572872 | tf_op jit(solution)/shard_map/ppermute | solution.py:30
  35.5 0.6 copy-start.6
  36.1 26.7 %all-to-all-start.1 = ((bf16[4,32,512]{2,1,0:T(8,128)(2,1)}), bf16[4,32,512]{2,1,0:T(8,128)(2,1)S(1)}, u32[]{:S(2)}, u32[]{:S(2)}) async-start(bf16[4,32,512]{2,1,0:T(8,128)(2,1)} %copy-done.6), calls=%async_computation.1 | async-start | bytes 262144 | tf_op jit(solution)/shard_map/all_to_all | solution.py:209
  54.6 0.7 copy-start.12
  55.3 21.2 %collective-permute-start.8 = (bf16[256,512]{1,0:T(8,128)(2,1)}, bf16[256,512]{1,0:T(8,128)(2,1)}, u32[]{:S(2)}, u32[]{:S(2)}) collective-permute-start(bf16[256,512]{1,0:T(8,128)(2,1)} %get-tuple-element.22), channel_id=1, source_target_pairs={{0,12},{4,0},{8,4},{12,8},{1,13},{5,1},{9,5},{13,9},{2,14},{6,2},{... | collective-permute-start | bytes 786440 | tf_op jit(solution)/shard_map/ppermute | solution.py:30
  57.8 18.8 %collective-permute-start.9 = (bf16[256,512]{1,0:T(8,128)(2,1)}, bf16[256,512]{1,0:T(8,128)(2,1)}, u32[]{:S(2)}, u32[]{:S(2)}) collective-permute-start(bf16[256,512]{1,0:T(8,128)(2,1)} %get-tuple-element.23), channel_id=1, source_target_pairs={{0,8},{4,12},{8,0},{12,4},{1,9},{5,13},{9,1},{13,5},{2,10},{6,14},... | collective-permute-start | bytes 786440 | tf_op jit(solution)/shard_map/ppermute | solution.py:30
  60.9 15.6 %collective-permute-start.7 = (bf16[256,512]{1,0:T(8,128)(2,1)}, bf16[256,512]{1,0:T(8,128)(2,1)}, u32[]{:S(2)}, u32[]{:S(2)}) collective-permute-start(bf16[256,512]{1,0:T(8,128)(2,1)} %get-tuple-element.18.refs_5_.rest_0_), channel_id=1, source_target_pairs={{0,4},{4,8},{8,12},{12,0},{1,5},{5,9},{9,13},{13,1},{2,6},{6,10},{... | collective-permute-start | bytes 786440 | tf_op jit(solution)/shard_map/ppermute | solution.py:30
  63.6 16.5 %all-to-all-start.2 = ((bf16[8,32,512]{2,1,0:T(8,128)(2,1)}), bf16[8,32,512]{2,1,0:T(8,128)(2,1)}, u32[]{:S(2)}, u32[]{:S(2)}) async-start(bf16[8,32,512]{2,1,0:T(8,128)(2,1)} %far_sum.1), calls=%async_computation.2 | async-start | bytes 524288 | tf_op jit(solution)/shard_map/all_to_all | solution.py:224
  67.6 8.9 %copy-start.5 = (bf16[1,256,512]{2,1,0:T(8,128)(2,1)S(1)}, bf16[1,256,512]{2,1,0:T(8,128)(2,1)}, u32[]{:S(2)}) copy-start(bf16[1,256,512]{2,1,0:T(8,128)(2,1)} %weight.3) | copy-start | bytes 786436
  67.6 8.9 %copy-start.10 = (bf16[1,256,512]{2,1,0:T(8,128)(2,1)S(1)}, bf16[1,256,512]{2,1,0:T(8,128)(2,1)}, u32[]{:S(2)}) copy-start(bf16[1,256,512]{2,1,0:T(8,128)(2,1)} %adam_first.1) | copy-start | bytes 786436
  67.7 8.9 %copy-start.11 = (bf16[1,256,512]{2,1,0:T(8,128)(2,1)S(1)}, bf16[1,256,512]{2,1,0:T(8,128)(2,1)}, u32[]{:S(2)}) copy-start(bf16[1,256,512]{2,1,0:T(8,128)(2,1)} %adam_second.1) | copy-start | bytes 786436
  67.7 8.9 %copy-start.13 = (bf16[256,512]{1,0:T(8,128)(2,1)S(1)}, bf16[256,512]{1,0:T(8,128)(2,1)}, u32[]{:S(2)}) copy-start(bf16[256,512]{1,0:T(8,128)(2,1)} %copy-done.12) | copy-start | bytes 786436
  70.2 8.6 %collective-permute-start.6 = (bf16[192,2048]{1,0:T(8,128)(2,1)S(1)}, bf16[192,2048]{1,0:T(8,128)(2,1)S(1)}, u32[]{:S(2)}, u32[]{:S(2)}) collective-permute-start(bf16[192,2048]{1,0:T(8,128)(2,1)S(1)} %get-tuple-element.20), channel_id=1, source_target_pairs={{0,1},{1,0},{2,3},{3,2},{4,5},{5,4},{6,7},{7,6},{8,9},{9,8},{10,11... | collective-permute-start | bytes 2359304 | tf_op jit(solution)/shard_map/ppermute | solution.py:30
  78.8 1.4 %copy-start.9 = (f32[1,1,8,512]{3,2,1,0:T(8,128)S(1)}, f32[1,1,8,512]{3,2,1,0:T(8,128)}, u32[]{:S(2)}) copy-start(f32[1,1,8,512]{3,2,1,0:T(8,128)} %momentum.3) | copy-start | bytes 49156

commit v4 on v3

--- a/solution.py
+++ b/solution.py
@@ -133,6 +133,10 @@
             mate[:, spot] = both[tokens:]
 
 
+def pair_kernel(own, across, _, out):
+    out[0], out[1] = own[...], across[...]
+
+
 def join_kernel(own, mate, *rest):
     out = rest[-1]
     core = lax.axis_index("core")
@@ -201,12 +205,12 @@
     keep = call(kept_kernel, (acts, cot, other, came), [shaped(256, 512)] * 4, "kept_terms", weight=1000000000)
     terms = [keep[0]] + [permute(keep[s], "x", 4, s) for s in (1, 3, 2)]
 
-    pair = jnp.stack([weight, across])
+    summed = call(functools.partial(spread_kernel, 1.0), (parts,), shaped(4, 32, 512), "near_sum")
+    pair = call(pair_kernel, (weight, across, summed), shaped(2, 256, 512), "pair", loose=1)
     pairs = [pair] + [permute(pair, "x", 4, s) for s in (1, 3, 2)]
     pairs = [pairs[0], pairs[1], pairs[3], pairs[2]]
 
-    parts = call(functools.partial(spread_kernel, 1.0), (parts,), shaped(4, 32, 512), "near_sum")
-    parts = lax.all_to_all(parts, "zhi", 0, 0, tiled=True)
+    parts = lax.all_to_all(summed, "zhi", 0, 0, tiled=True)
     mine, sent = call(
         input_kernel,
         (cot, other, *pairs, parts, keep[1]),

time: 82.7 us -> 81.2 us (0.982)
  other arithmetic: 1 us -> 0 us
    all_to_all x1, starting transfers between devices: 14.3 us -> 12.9 us  [shards(): parts = lax.all_to_all(summed, 'zhi', 0, 0, tiled=True)]
    ppermute x10, starting transfers between devices: 33.8 us -> 35 us  [permute(): lax.ppermute(array, axis, [(i, (i + shift) % size) for i in range(size)])]
    another operation x1 -> x0, other arithmetic: 1 us -> none  [shards(): pair = jnp.stack([weight, across])]
    pallas_call x10 -> x11, Pallas kernels: 16.1 us -> 15.8 us  [call(): pl.pallas_call(kernel, in_specs=[pl.BlockSpec(memory_space=pltpu.VMEM)] *...]
    unnamed x28 -> x24, local copies, waits for them, and re-layouts: 1.41 us -> 1.7 us
  transfers between devices with their start and end apart: 13 -> 13, of which waited for: 2 -> 2; matrix products, arithmetic and copies ran while one was open for 1% -> 0% of each run, Pallas kernels for 15% -> 16%
where the time goes in v4:
time: 81.2 us; the launch traced here: 80.4 us
  starting transfers between devices  55.2 us (68%)
  Pallas kernels  15.8 us (19%)
  waiting for transfers between devices  6.8 us (8%)
  local copies, waits for them, and re-layouts  1.7 us (2%)
  between operations  0.94 us (1%)
    ppermute x10, starting transfers between devices, permute(): lax.ppermute(array, axis, [(i, (i + shift) % size) for i in range(size)])  35 us
    pallas_call x11, Pallas kernels, call(): pl.pallas_call(kernel, in_specs=[pl.BlockSpec(memory_space=pltpu.VMEM)] *...  15.8 us
    all_to_all x1, starting transfers between devices, shards(): parts = lax.all_to_all(summed, 'zhi', 0, 0, tiled=True)  12.9 us
    ppermute x10, waiting for transfers between devices, permute(): lax.ppermute(array, axis, [(i, (i + shift) % size) for i in range(size)])  6.8 us
    all_to_all x1, starting transfers between devices, shards(): rows = lax.all_to_all(rows, near, 0, 0, tiled=True).reshape(256, 512)  3.83 us
    all_to_all x1, starting transfers between devices, shards(): parts = lax.all_to_all(blocks.reshape(8, 32, 512), near, 0, 0, tiled=True)  3.41 us
    unnamed x24, local copies, waits for them, and re-layouts  1.7 us
  transfers between devices with their start and end apart: 13, of which 2 were waited for; matrix products, arithmetic and copies ran while one was open for 0% of the time, Pallas kernels for 16%

profile of v4, /device:TPU:1, one launch (start us, length us, event | category | flops | bytes accessed | tf_op | source)
XLA Modules:
  0.0 80.4 jit_solution(7392932722970947166)
XLA Ops:
  0.6 0.0 copy-start.1
  0.6 0.0 copy-start
  0.7 0.0 copy-start.2
  0.7 0.0 copy-start.6
  0.7 0.0 copy-start.5
  0.7 2.5 %pack.1 = bf16[192,2560]{1,0:T(8,128)(2,1)} custom-call(bf16[192,4096]{1,0:T(8,128)(2,1)} %acts.5, bf16[192,512]{1,0:T(8,128)(2,1)} %cot.7), custom_call_target="tpu_custom_call" | custom-call | flops 500000000 | bytes 262144 | tf_op jit(solution)/shard_map/pack/pallas_call | solution.py:44
  3.1 8.8 %collective-permute-start = (bf16[192,2560]{1,0:T(8,128)(2,1)}, bf16[192,2560]{1,0:T(8,128)(2,1)S(1)}, u32[]{:S(2)}, u32[]{:S(2)}) collective-permute-start(bf16[192,2560]{1,0:T(8,128)(2,1)} %pack.1), channel_id=1, source_target_pairs={{0,1},{1,0},{2,3},{3,2},{4,5},{5,4},{6,7},{7,6},{8,9},{9,8},{10,11... | collective-permute-start | bytes 2949128 | tf_op jit(solution)/shard_map/ppermute | solution.py:30
  11.9 0.0 copy-done.2
  11.9 1.9 %collective-permute-start.1 = (bf16[256,512]{1,0:T(8,128)(2,1)S(1)}, bf16[256,512]{1,0:T(8,128)(2,1)S(1)}, u32[]{:S(2)}, u32[]{:S(2)}) collective-permute-start(bf16[256,512]{1,0:T(8,128)(2,1)S(1)} %bitcast.3), channel_id=1, source_target_pairs={{0,2},{2,0},{1,3},{3,1},{4,6},{6,4},{5,7},{7,5},{8,10},{10,8},{9,1... | collective-permute-start | bytes 786440 | tf_op jit(solution)/shard_map/ppermute | solution.py:30
  13.9 0.0 copy-done.6
  13.9 0.0 copy-done.5
  13.9 0.7 fold_outer_state.1.rest_0_
  14.6 3.4 %all-to-all-start = ((bf16[8,32,512]{2,1,0:T(8,128)(2,1)}), bf16[8,32,512]{2,1,0:T(8,128)(2,1)S(1)}, u32[]{:S(2)}, u32[]{:S(2)}) async-start(bf16[8,32,512]{2,1,0:T(8,128)(2,1)} %bitcast.1), calls=%async_computation | async-start | bytes 524288 | tf_op jit(solution)/shard_map/all_to_all | solution.py:199
  18.1 5.2 %collective-permute-done.1.across.rest_1_ = bf16[256,512]{1,0:T(8,128)(2,1)S(1)} collective-permute-done((bf16[256,512]{1,0:T(8,128)(2,1)S(1)}, bf16[256,512]{1,0:T(8,128)(2,1)S(1)}, u32[]{:S(2)}, u32[]{:S(2)}) %collective-permute-start.1) | collective-permute-done | bytes 262176 | tf_op jit(solution)/shard_map/ppermute | solution.py:30
  23.3 0.0 collective-permute-done.other
  23.3 0.0 copy-done.1
  23.3 0.0 copy-done
  23.3 1.7 %sent_terms.1 = bf16[4,256,512]{2,1,0:T(8,128)(2,1)} custom-call(bf16[192,4096]{1,0:T(8,128)(2,1)S(1)} %copy-done, bf16[192,512]{1,0:T(8,128)(2,1)S(1)} %copy-done.1, bf16[192,2560]{1,0:T(8,128)(2,1)S(1)} %collective-permute-done.other, bf16[256,512]{1,0:T(8,128)(2,1)} %fold_outer_state.1.rest_0_, bf16[256,512]{1,0:T(8,128)(2,1)S(1)} %collective-permute-done.1.across.rest_1_), custom_call_target="tpu_custom_call" | custom-call | flops 500000000 | bytes 262144 | tf_op jit(solution)/shard_map/sent_terms/pallas_call | solution.py:44
  25.0 2.1 %collective-permute-start.5 = (bf16[4,256,512]{2,1,0:T(8,128)(2,1)}, bf16[4,256,512]{2,1,0:T(8,128)(2,1)}, u32[]{:S(2)}, u32[]{:S(2)}) collective-permute-start(bf16[4,256,512]{2,1,0:T(8,128)(2,1)} %sent_terms.1), channel_id=1, source_target_pairs={{0,2},{2,0},{1,3},{3,1},{4,6},{6,4},{5,7},{7,5},{8,10},{10,8},{9,1... | collective-permute-start | bytes 3145736 | tf_op jit(solution)/shard_map/ppermute | solution.py:30
  27.1 0.0 all-to-all-done.parts
  27.2 0.7 near_sum.1._
  27.8 0.0 copy-start.3
  27.8 0.9 %copy-done.3 = bf16[1,256,512]{2,1,0:T(8,128)(2,1)S(1)} copy-done((bf16[1,256,512]{2,1,0:T(8,128)(2,1)S(1)}, bf16[1,256,512]{2,1,0:T(8,128)(2,1)}, u32[]{:S(2)}) %copy-start.3) | copy-done | bytes 262168
  28.8 3.6 %collective-permute-start.4 = (bf16[2,256,512]{2,1,0:T(8,128)(2,1)S(1)}, bf16[2,256,512]{2,1,0:T(8,128)(2,1)}, u32[]{:S(2)}, u32[]{:S(2)}) collective-permute-start(bf16[2,256,512]{2,1,0:T(8,128)(2,1)S(1)} %pair.1.refs_0_), channel_id=1, source_target_pairs={{0,12},{4,0},{8,4},{12,8},{1,13},{5,1},{9,5},{13,9},{2,14},{6,2},{... | collective-permute-start | bytes 1572872 | tf_op jit(solution)/shard_map/ppermute | solution.py:30
  32.5 2.4 %collective-permute-start.3 = (bf16[2,256,512]{2,1,0:T(8,128)(2,1)S(1)}, bf16[2,256,512]{2,1,0:T(8,128)(2,1)}, u32[]{:S(2)}, u32[]{:S(2)}) collective-permute-start(bf16[2,256,512]{2,1,0:T(8,128)(2,1)S(1)} %pair.1.refs_0_), channel_id=1, source_target_pairs={{0,8},{4,12},{8,0},{12,4},{1,9},{5,13},{9,1},{13,5},{2,10},{6,14},... | collective-permute-start | bytes 1572872 | tf_op jit(solution)/shard_map/ppermute | solution.py:30
  34.9 2.5 %collective-permute-start.2 = (bf16[2,256,512]{2,1,0:T(8,128)(2,1)S(1)}, bf16[2,256,512]{2,1,0:T(8,128)(2,1)}, u32[]{:S(2)}, u32[]{:S(2)}) collective-permute-start(bf16[2,256,512]{2,1,0:T(8,128)(2,1)S(1)} %pair.1.refs_0_), channel_id=1, source_target_pairs={{0,4},{4,8},{8,12},{12,0},{1,5},{5,9},{9,13},{13,1},{2,6},{6,10},{... | collective-permute-start | bytes 1572872 | tf_op jit(solution)/shard_map/ppermute | solution.py:30
  37.4 12.9 %all-to-all-start.1 = ((bf16[4,32,512]{2,1,0:T(8,128)(2,1)}), bf16[4,32,512]{2,1,0:T(8,128)(2,1)S(1)}, u32[]{:S(2)}, u32[]{:S(2)}) async-start(bf16[4,32,512]{2,1,0:T(8,128)(2,1)} %near_sum.1._), calls=%async_computation.1 | async-start | bytes 262144 | tf_op jit(solution)/shard_map/all_to_all | solution.py:213
  50.3 1.6 %collective-permute-done.5.came = bf16[4,256,512]{2,1,0:T(8,128)(2,1)} collective-permute-done((bf16[4,256,512]{2,1,0:T(8,128)(2,1)}, bf16[4,256,512]{2,1,0:T(8,128)(2,1)}, u32[]{:S(2)}, u32[]{:S(2)}) %collective-permute-start.5) | collective-permute-done | bytes 1048608 | tf_op jit(solution)/shard_map/ppermute | solution.py:30
  51.9 2.7 %kept_terms.1 = (bf16[256,512]{1,0:T(8,128)(2,1)S(1)}, bf16[256,512]{1,0:T(8,128)(2,1)}, bf16[256,512]{1,0:T(8,128)(2,1)}, bf16[256,512]{1,0:T(8,128)(2,1)}) custom-call(bf16[192,4096]{1,0:T(8,128)(2,1)S(1)} %copy-done, bf16[192,512]{1,0:T(8,128)(2,1)S(1)} %copy-done.1, bf16[192,2560]{1,0:T(8,128)(2,1)S(1)} %collective-permute-done.other, ...), custom_call_target="tpu_custom_call" | custom-call | flops 1000000000 | bytes 262144 | tf_op jit(solution)/shard_map/kept_terms/pallas_call | solution.py:44
  54.6 0.0 copy-start.10
  54.6 0.7 copy-done.10
  55.3 2.4 %collective-permute-start.8 = (bf16[256,512]{1,0:T(8,128)(2,1)}, bf16[256,512]{1,0:T(8,128)(2,1)S(1)}, u32[]{:S(2)}, u32[]{:S(2)}) collective-permute-start(bf16[256,512]{1,0:T(8,128)(2,1)} %get-tuple-element.22), channel_id=1, source_target_pairs={{0,12},{4,0},{8,4},{12,8},{1,13},{5,1},{9,5},{13,9},{2,14},{6,2},{... | collective-permute-start | bytes 786440 | tf_op jit(solution)/shard_map/ppermute | solution.py:30
  57.7 3.2 %collective-permute-start.9 = (bf16[256,512]{1,0:T(8,128)(2,1)}, bf16[256,512]{1,0:T(8,128)(2,1)}, u32[]{:S(2)}, u32[]{:S(2)}) collective-permute-start(bf16[256,512]{1,0:T(8,128)(2,1)} %get-tuple-element.23), channel_id=1, source_target_pairs={{0,8},{4,12},{8,0},{12,4},{1,9},{5,13},{9,1},{13,5},{2,10},{6,14},... | collective-permute-start | bytes 786440 | tf_op jit(solution)/shard_map/ppermute | solution.py:30
  60.9 0.0 collective-permute-done.4.refs_3_
  60.9 1.9 %collective-permute-start.7 = (bf16[256,512]{1,0:T(8,128)(2,1)}, bf16[256,512]{1,0:T(8,128)(2,1)}, u32[]{:S(2)}, u32[]{:S(2)}) collective-permute-start(bf16[256,512]{1,0:T(8,128)(2,1)} %get-tuple-element.18.refs_5_.rest_0_), channel_id=1, source_target_pairs={{0,4},{4,8},{8,12},{12,0},{1,5},{5,9},{9,13},{13,1},{2,6},{6,10},{... | collective-permute-start | bytes 786440 | tf_op jit(solution)/shard_map/ppermute | solution.py:30
  62.8 0.0 all-to-all-done.1.refs_4_.parts
  62.8 0.7 far_sum.1
  63.6 3.8 %all-to-all-start.2 = ((bf16[8,32,512]{2,1,0:T(8,128)(2,1)}), bf16[8,32,512]{2,1,0:T(8,128)(2,1)S(1)}, u32[]{:S(2)}, u32[]{:S(2)}) async-start(bf16[8,32,512]{2,1,0:T(8,128)(2,1)} %far_sum.1), calls=%async_computation.2 | async-start | bytes 524288 | tf_op jit(solution)/shard_map/all_to_all | solution.py:228
  67.4 0.0 copy-start.4
  67.4 0.0 copy-start.8
  67.4 0.0 copy-start.9
  67.4 0.0 copy-start.11
  67.4 0.0 collective-permute-done.3.refs_2_
  67.5 0.0 collective-permute-done.2.refs_1_
  67.5 2.5 %input_grad_columns.1 = (bf16[192,2048]{1,0:T(8,128)(2,1)S(1)}, bf16[192,2048]{1,0:T(8,128)(2,1)S(1)}) custom-call(bf16[192,512]{1,0:T(8,128)(2,1)S(1)} %copy-done.1, bf16[192,2560]{1,0:T(8,128)(2,1)S(1)} %collective-permute-done.other, bf16[2,256,512]{2,1,0:T(8,128)(2,1)S(1)} %pair.1.refs_0_, bf16[2,256,512]{2,1,0:T(8,128)(2,1)} %collective-permute-done.2.refs_1_, ...), custom_call_target="tpu_custom_call" | custom-call | bytes 262144 | tf_op jit(solution)/shard_map/input_grad_columns/pallas_call | solution.py:44
  69.9 6.1 %collective-permute-start.6 = (bf16[192,2048]{1,0:T(8,128)(2,1)S(1)}, bf16[192,2048]{1,0:T(8,128)(2,1)S(1)}, u32[]{:S(2)}, u32[]{:S(2)}) collective-permute-start(bf16[192,2048]{1,0:T(8,128)(2,1)S(1)} %get-tuple-element.20), channel_id=1, source_target_pairs={{0,1},{1,0},{2,3},{3,2},{4,5},{5,4},{6,7},{7,6},{8,9},{9,8},{10,11... | collective-permute-start | bytes 2359304 | tf_op jit(solution)/shard_map/ppermute | solution.py:30
  76.1 0.0 collective-permute-done.8.t2
  76.1 0.0 collective-permute-done.9.t3
  76.1 0.0 collective-permute-done.7.t1
  76.1 0.0 copy-done.4
  76.1 0.0 copy-done.8
  76.1 0.0 copy-done.9
  76.1 0.0 copy-done.11
  76.2 2.1 %adam.1 = (f32[256,512]{1,0:T(8,128)S(1)}, bf16[1,256,512]{2,1,0:T(8,128)(2,1)}, bf16[1,256,512]{2,1,0:T(8,128)(2,1)}) custom-call(bf16[256,512]{1,0:T(8,128)(2,1)S(1)} %copy-done.11, bf16[256,512]{1,0:T(8,128)(2,1)} %collective-permute-done.7.t1, bf16[256,512]{1,0:T(8,128)(2,1)S(1)} %collective-permute-done.8.t2, ...), custom_call_target="tpu_custom_call" | custom-call | flops 8000000000 | bytes 262144 | tf_op jit(solution)/shard_map/adam/pallas_call | solution.py:44
  78.2 0.0 collective-permute-done.6.mate
  78.3 0.0 copy-start.7
  78.3 1.3 %input_grad.1 = bf16[192,4096]{1,0:T(8,128)(2,1)} custom-call(bf16[192,2048]{1,0:T(8,128)(2,1)S(1)} %get-tuple-element.19.own, bf16[192,2048]{1,0:T(8,128)(2,1)S(1)} %collective-permute-done.6.mate), custom_call_target="tpu_custom_call" | custom-call | bytes 262144 | tf_op jit(solution)/shard_map/input_grad/pallas_call | solution.py:44
  79.6 0.0 all-to-all-done.2
  79.6 0.0 copy-done.7
  79.6 0.8 mix.1
  (1 shorter events, 0.0 us)
Async XLA Ops:
  0.6 22.6 %copy-start.1 = (bf16[192,512]{1,0:T(8,128)(2,1)S(1)}, bf16[192,512]{1,0:T(8,128)(2,1)}, u32[]{:S(2)}) copy-start(bf16[192,512]{1,0:T(8,128)(2,1)} %cot.7) | copy-start | bytes 589828
  0.6 22.6 %copy-start = (bf16[192,4096]{1,0:T(8,128)(2,1)S(1)}, bf16[192,4096]{1,0:T(8,128)(2,1)}, u32[]{:S(2)}) copy-start(bf16[192,4096]{1,0:T(8,128)(2,1)} %acts.5) | copy-start | bytes 4718596
  0.7 11.3 %copy-start.2 = (bf16[1,256,512]{2,1,0:T(8,128)(2,1)S(1)}, bf16[1,256,512]{2,1,0:T(8,128)(2,1)}, u32[]{:S(2)}) copy-start(bf16[1,256,512]{2,1,0:T(8,128)(2,1)} %weight.3) | copy-start | bytes 786436
  0.7 13.2 %copy-start.6 = (f32[1,1,8,512]{3,2,1,0:T(8,128)S(1)}, f32[1,1,8,512]{3,2,1,0:T(8,128)}, u32[]{:S(2)}) copy-start(f32[1,1,8,512]{3,2,1,0:T(8,128)} %momentum.3) | copy-start | bytes 49156
  0.7 13.2 %copy-start.5 = (f32[1,1,8,512]{3,2,1,0:T(8,128)S(1)}, f32[1,1,8,512]{3,2,1,0:T(8,128)}, u32[]{:S(2)}) copy-start(f32[1,1,8,512]{3,2,1,0:T(8,128)} %globe.3) | copy-start | bytes 49156
  3.1 20.1 %collective-permute-start = (bf16[192,2560]{1,0:T(8,128)(2,1)}, bf16[192,2560]{1,0:T(8,128)(2,1)S(1)}, u32[]{:S(2)}, u32[]{:S(2)}) collective-permute-start(bf16[192,2560]{1,0:T(8,128)(2,1)} %pack.1), channel_id=1, source_target_pairs={{0,1},{1,0},{2,3},{3,2},{4,5},{5,4},{6,7},{7,6},{8,9},{9,8},{10,11... | collective-permute-start | bytes 2949128 | tf_op jit(solution)/shard_map/ppermute | solution.py:30
  11.9 11.3 %collective-permute-start.1 = (bf16[256,512]{1,0:T(8,128)(2,1)S(1)}, bf16[256,512]{1,0:T(8,128)(2,1)S(1)}, u32[]{:S(2)}, u32[]{:S(2)}) collective-permute-start(bf16[256,512]{1,0:T(8,128)(2,1)S(1)} %bitcast.3), channel_id=1, source_target_pairs={{0,2},{2,0},{1,3},{3,1},{4,6},{6,4},{5,7},{7,5},{8,10},{10,8},{9,1... | collective-permute-start | bytes 786440 | tf_op jit(solution)/shard_map/ppermute | solution.py:30
  14.6 12.5 %all-to-all-start = ((bf16[8,32,512]{2,1,0:T(8,128)(2,1)}), bf16[8,32,512]{2,1,0:T(8,128)(2,1)S(1)}, u32[]{:S(2)}, u32[]{:S(2)}) async-start(bf16[8,32,512]{2,1,0:T(8,128)(2,1)} %bitcast.1), calls=%async_computation | async-start | bytes 524288 | tf_op jit(solution)/shard_map/all_to_all | solution.py:199
  25.0 26.9 %collective-permute-start.5 = (bf16[4,256,512]{2,1,0:T(8,128)(2,1)}, bf16[4,256,512]{2,1,0:T(8,128)(2,1)}, u32[]{:S(2)}, u32[]{:S(2)}) collective-permute-start(bf16[4,256,512]{2,1,0:T(8,128)(2,1)} %sent_terms.1), channel_id=1, source_target_pairs={{0,2},{2,0},{1,3},{3,1},{4,6},{6,4},{5,7},{7,5},{8,10},{10,8},{9,1... | collective-permute-start | bytes 3145736 | tf_op jit(solution)/shard_map/ppermute | solution.py:30
  27.8 0.9 %copy-start.3 = (bf16[1,256,512]{2,1,0:T(8,128)(2,1)S(1)}, bf16[1,256,512]{2,1,0:T(8,128)(2,1)}, u32[]{:S(2)}) copy-start(bf16[1,256,512]{2,1,0:T(8,128)(2,1)} %weight.3) | copy-start | bytes 786436
  28.8 32.0 %collective-permute-start.4 = (bf16[2,256,512]{2,1,0:T(8,128)(2,1)S(1)}, bf16[2,256,512]{2,1,0:T(8,128)(2,1)}, u32[]{:S(2)}, u32[]{:S(2)}) collective-permute-start(bf16[2,256,512]{2,1,0:T(8,128)(2,1)S(1)} %pair.1.refs_0_), channel_id=1, source_target_pairs={{0,12},{4,0},{8,4},{12,8},{1,13},{5,1},{9,5},{13,9},{2,14},{6,2},{... | collective-permute-start | bytes 1572872 | tf_op jit(solution)/shard_map/ppermute | solution.py:30
  32.5 35.0 %collective-permute-start.3 = (bf16[2,256,512]{2,1,0:T(8,128)(2,1)S(1)}, bf16[2,256,512]{2,1,0:T(8,128)(2,1)}, u32[]{:S(2)}, u32[]{:S(2)}) collective-permute-start(bf16[2,256,512]{2,1,0:T(8,128)(2,1)S(1)} %pair.1.refs_0_), channel_id=1, source_target_pairs={{0,8},{4,12},{8,0},{12,4},{1,9},{5,13},{9,1},{13,5},{2,10},{6,14},... | collective-permute-start | bytes 1572872 | tf_op jit(solution)/shard_map/ppermute | solution.py:30
  34.9 32.6 %collective-permute-start.2 = (bf16[2,256,512]{2,1,0:T(8,128)(2,1)S(1)}, bf16[2,256,512]{2,1,0:T(8,128)(2,1)}, u32[]{:S(2)}, u32[]{:S(2)}) collective-permute-start(bf16[2,256,512]{2,1,0:T(8,128)(2,1)S(1)} %pair.1.refs_0_), channel_id=1, source_target_pairs={{0,4},{4,8},{8,12},{12,0},{1,5},{5,9},{9,13},{13,1},{2,6},{6,10},{... | collective-permute-start | bytes 1572872 | tf_op jit(solution)/shard_map/ppermute | solution.py:30
  37.4 25.4 %all-to-all-start.1 = ((bf16[4,32,512]{2,1,0:T(8,128)(2,1)}), bf16[4,32,512]{2,1,0:T(8,128)(2,1)S(1)}, u32[]{:S(2)}, u32[]{:S(2)}) async-start(bf16[4,32,512]{2,1,0:T(8,128)(2,1)} %near_sum.1._), calls=%async_computation.1 | async-start | bytes 262144 | tf_op jit(solution)/shard_map/all_to_all | solution.py:213
  54.6 0.7 copy-start.10
  55.3 20.8 %collective-permute-start.8 = (bf16[256,512]{1,0:T(8,128)(2,1)}, bf16[256,512]{1,0:T(8,128)(2,1)S(1)}, u32[]{:S(2)}, u32[]{:S(2)}) collective-permute-start(bf16[256,512]{1,0:T(8,128)(2,1)} %get-tuple-element.22), channel_id=1, source_target_pairs={{0,12},{4,0},{8,4},{12,8},{1,13},{5,1},{9,5},{13,9},{2,14},{6,2},{... | collective-permute-start | bytes 786440 | tf_op jit(solution)/shard_map/ppermute | solution.py:30
  57.7 18.4 %collective-permute-start.9 = (bf16[256,512]{1,0:T(8,128)(2,1)}, bf16[256,512]{1,0:T(8,128)(2,1)}, u32[]{:S(2)}, u32[]{:S(2)}) collective-permute-start(bf16[256,512]{1,0:T(8,128)(2,1)} %get-tuple-element.23), channel_id=1, source_target_pairs={{0,8},{4,12},{8,0},{12,4},{1,9},{5,13},{9,1},{13,5},{2,10},{6,14},... | collective-permute-start | bytes 786440 | tf_op jit(solution)/shard_map/ppermute | solution.py:30
  60.9 15.2 %collective-permute-start.7 = (bf16[256,512]{1,0:T(8,128)(2,1)}, bf16[256,512]{1,0:T(8,128)(2,1)}, u32[]{:S(2)}, u32[]{:S(2)}) collective-permute-start(bf16[256,512]{1,0:T(8,128)(2,1)} %get-tuple-element.18.refs_5_.rest_0_), channel_id=1, source_target_pairs={{0,4},{4,8},{8,12},{12,0},{1,5},{5,9},{9,13},{13,1},{2,6},{6,10},{... | collective-permute-start | bytes 786440 | tf_op jit(solution)/shard_map/ppermute | solution.py:30
  63.6 16.0 %all-to-all-start.2 = ((bf16[8,32,512]{2,1,0:T(8,128)(2,1)}), bf16[8,32,512]{2,1,0:T(8,128)(2,1)S(1)}, u32[]{:S(2)}, u32[]{:S(2)}) async-start(bf16[8,32,512]{2,1,0:T(8,128)(2,1)} %far_sum.1), calls=%async_computation.2 | async-start | bytes 524288 | tf_op jit(solution)/shard_map/all_to_all | solution.py:228
  67.4 8.7 %copy-start.4 = (bf16[1,256,512]{2,1,0:T(8,128)(2,1)S(1)}, bf16[1,256,512]{2,1,0:T(8,128)(2,1)}, u32[]{:S(2)}) copy-start(bf16[1,256,512]{2,1,0:T(8,128)(2,1)} %weight.3) | copy-start | bytes 786436
  67.4 8.7 %copy-start.8 = (bf16[1,256,512]{2,1,0:T(8,128)(2,1)S(1)}, bf16[1,256,512]{2,1,0:T(8,128)(2,1)}, u32[]{:S(2)}) copy-start(bf16[1,256,512]{2,1,0:T(8,128)(2,1)} %adam_first.1) | copy-start | bytes 786436
  67.4 8.7 %copy-start.9 = (bf16[1,256,512]{2,1,0:T(8,128)(2,1)S(1)}, bf16[1,256,512]{2,1,0:T(8,128)(2,1)}, u32[]{:S(2)}) copy-start(bf16[1,256,512]{2,1,0:T(8,128)(2,1)} %adam_second.1) | copy-start | bytes 786436
  67.4 8.7 %copy-start.11 = (bf16[256,512]{1,0:T(8,128)(2,1)S(1)}, bf16[256,512]{1,0:T(8,128)(2,1)}, u32[]{:S(2)}) copy-start(bf16[256,512]{1,0:T(8,128)(2,1)} %copy-done.10) | copy-start | bytes 786436
  69.9 8.3 %collective-permute-start.6 = (bf16[192,2048]{1,0:T(8,128)(2,1)S(1)}, bf16[192,2048]{1,0:T(8,128)(2,1)S(1)}, u32[]{:S(2)}, u32[]{:S(2)}) collective-permute-start(bf16[192,2048]{1,0:T(8,128)(2,1)S(1)} %get-tuple-element.20), channel_id=1, source_target_pairs={{0,1},{1,0},{2,3},{3,2},{4,5},{5,4},{6,7},{7,6},{8,9},{9,8},{10,11... | collective-permute-start | bytes 2359304 | tf_op jit(solution)/shard_map/ppermute | solution.py:30
  78.3 1.4 %copy-start.7 = (f32[1,1,8,512]{3,2,1,0:T(8,128)S(1)}, f32[1,1,8,512]{3,2,1,0:T(8,128)}, u32[]{:S(2)}) copy-start(f32[1,1,8,512]{3,2,1,0:T(8,128)} %momentum.3) | copy-start | bytes 49156

commit v5 on v4

--- a/solution.py
+++ b/solution.py
@@ -203,7 +203,7 @@
     came = permute(send, "yhi", 2, 1)
 
     keep = call(kept_kernel, (acts, cot, other, came), [shaped(256, 512)] * 4, "kept_terms", weight=1000000000)
-    terms = [keep[0]] + [permute(keep[s], "x", 4, s) for s in (1, 3, 2)]
+    terms = [keep[0]] + [permute(keep[s], "x", 4, s) for s in (2, 1, 3)]
 
     summed = call(functools.partial(spread_kernel, 1.0), (parts,), shaped(4, 32, 512), "near_sum")
     pair = call(pair_kernel, (weight, across, summed), shaped(2, 256, 512), "pair", loose=1)

time: 81.2 us -> 81.2 us (level)
  no operation moved by 1% of the time
where the time goes in v5:
time: 81.2 us; the launch traced here: 80.4 us
  starting transfers between devices  55.2 us (68%)
  Pallas kernels  15.8 us (19%)
  waiting for transfers between devices  6.8 us (8%)
  local copies, waits for them, and re-layouts  1.7 us (2%)
  between operations  0.94 us (1%)
    ppermute x10, starting transfers between devices, permute(): lax.ppermute(array, axis, [(i, (i + shift) % size) for i in range(size)])  35 us
    pallas_call x11, Pallas kernels, call(): pl.pallas_call(kernel, in_specs=[pl.BlockSpec(memory_space=pltpu.VMEM)] *...  15.8 us
    all_to_all x1, starting transfers between devices, shards(): parts = lax.all_to_all(summed, 'zhi', 0, 0, tiled=True)  12.9 us
    ppermute x10, waiting for transfers between devices, permute(): lax.ppermute(array, axis, [(i, (i + shift) % size) for i in range(size)])  6.8 us
    all_to_all x1, starting transfers between devices, shards(): rows = lax.all_to_all(rows, near, 0, 0, tiled=True).reshape(256, 512)  3.83 us
    all_to_all x1, starting transfers between devices, shards(): parts = lax.all_to_all(blocks.reshape(8, 32, 512), near, 0, 0, tiled=True)  3.41 us
    unnamed x24, local copies, waits for them, and re-layouts  1.7 us
  transfers between devices with their start and end apart: 13, of which 2 were waited for; matrix products, arithmetic and copies ran while one was open for 0% of the time, Pallas kernels for 16%

profile of v5, /device:TPU:1, one launch (start us, length us, event | category | flops | bytes accessed | tf_op | source)
XLA Modules:
  0.0 80.4 jit_solution(13656594487527064766)
XLA Ops:
  0.6 0.0 copy-start.1
  0.6 0.0 copy-start
  0.7 0.0 copy-start.2
  0.7 0.0 copy-start.6
  0.7 0.0 copy-start.5
  0.7 2.5 %pack.1 = bf16[192,2560]{1,0:T(8,128)(2,1)} custom-call(bf16[192,4096]{1,0:T(8,128)(2,1)} %acts.5, bf16[192,512]{1,0:T(8,128)(2,1)} %cot.7), custom_call_target="tpu_custom_call" | custom-call | flops 500000000 | bytes 262144 | tf_op jit(solution)/shard_map/pack/pallas_call | solution.py:44
  3.1 8.8 %collective-permute-start = (bf16[192,2560]{1,0:T(8,128)(2,1)}, bf16[192,2560]{1,0:T(8,128)(2,1)S(1)}, u32[]{:S(2)}, u32[]{:S(2)}) collective-permute-start(bf16[192,2560]{1,0:T(8,128)(2,1)} %pack.1), channel_id=1, source_target_pairs={{0,1},{1,0},{2,3},{3,2},{4,5},{5,4},{6,7},{7,6},{8,9},{9,8},{10,11... | collective-permute-start | bytes 2949128 | tf_op jit(solution)/shard_map/ppermute | solution.py:30
  11.9 0.0 copy-done.2
  11.9 1.9 %collective-permute-start.1 = (bf16[256,512]{1,0:T(8,128)(2,1)S(1)}, bf16[256,512]{1,0:T(8,128)(2,1)S(1)}, u32[]{:S(2)}, u32[]{:S(2)}) collective-permute-start(bf16[256,512]{1,0:T(8,128)(2,1)S(1)} %bitcast.3), channel_id=1, source_target_pairs={{0,2},{2,0},{1,3},{3,1},{4,6},{6,4},{5,7},{7,5},{8,10},{10,8},{9,1... | collective-permute-start | bytes 786440 | tf_op jit(solution)/shard_map/ppermute | solution.py:30
  13.9 0.0 copy-done.6
  13.9 0.0 copy-done.5
  13.9 0.7 fold_outer_state.1.rest_0_
  14.6 3.4 %all-to-all-start = ((bf16[8,32,512]{2,1,0:T(8,128)(2,1)}), bf16[8,32,512]{2,1,0:T(8,128)(2,1)S(1)}, u32[]{:S(2)}, u32[]{:S(2)}) async-start(bf16[8,32,512]{2,1,0:T(8,128)(2,1)} %bitcast.1), calls=%async_computation | async-start | bytes 524288 | tf_op jit(solution)/shard_map/all_to_all | solution.py:199
  18.1 5.2 %collective-permute-done.1.across.rest_1_ = bf16[256,512]{1,0:T(8,128)(2,1)S(1)} collective-permute-done((bf16[256,512]{1,0:T(8,128)(2,1)S(1)}, bf16[256,512]{1,0:T(8,128)(2,1)S(1)}, u32[]{:S(2)}, u32[]{:S(2)}) %collective-permute-start.1) | collective-permute-done | bytes 262176 | tf_op jit(solution)/shard_map/ppermute | solution.py:30
  23.3 0.0 collective-permute-done.other
  23.3 0.0 copy-done.1
  23.3 0.0 copy-done
  23.3 1.7 %sent_terms.1 = bf16[4,256,512]{2,1,0:T(8,128)(2,1)} custom-call(bf16[192,4096]{1,0:T(8,128)(2,1)S(1)} %copy-done, bf16[192,512]{1,0:T(8,128)(2,1)S(1)} %copy-done.1, bf16[192,2560]{1,0:T(8,128)(2,1)S(1)} %collective-permute-done.other, bf16[256,512]{1,0:T(8,128)(2,1)} %fold_outer_state.1.rest_0_, bf16[256,512]{1,0:T(8,128)(2,1)S(1)} %collective-permute-done.1.across.rest_1_), custom_call_target="tpu_custom_call" | custom-call | flops 500000000 | bytes 262144 | tf_op jit(solution)/shard_map/sent_terms/pallas_call | solution.py:44
  25.0 2.1 %collective-permute-start.5 = (bf16[4,256,512]{2,1,0:T(8,128)(2,1)}, bf16[4,256,512]{2,1,0:T(8,128)(2,1)}, u32[]{:S(2)}, u32[]{:S(2)}) collective-permute-start(bf16[4,256,512]{2,1,0:T(8,128)(2,1)} %sent_terms.1), channel_id=1, source_target_pairs={{0,2},{2,0},{1,3},{3,1},{4,6},{6,4},{5,7},{7,5},{8,10},{10,8},{9,1... | collective-permute-start | bytes 3145736 | tf_op jit(solution)/shard_map/ppermute | solution.py:30
  27.1 0.0 all-to-all-done.parts
  27.2 0.7 near_sum.1._
  27.8 0.0 copy-start.3
  27.8 0.9 %copy-done.3 = bf16[1,256,512]{2,1,0:T(8,128)(2,1)S(1)} copy-done((bf16[1,256,512]{2,1,0:T(8,128)(2,1)S(1)}, bf16[1,256,512]{2,1,0:T(8,128)(2,1)}, u32[]{:S(2)}) %copy-start.3) | copy-done | bytes 262168
  28.8 3.6 %collective-permute-start.4 = (bf16[2,256,512]{2,1,0:T(8,128)(2,1)S(1)}, bf16[2,256,512]{2,1,0:T(8,128)(2,1)}, u32[]{:S(2)}, u32[]{:S(2)}) collective-permute-start(bf16[2,256,512]{2,1,0:T(8,128)(2,1)S(1)} %pair.1.refs_0_), channel_id=1, source_target_pairs={{0,12},{4,0},{8,4},{12,8},{1,13},{5,1},{9,5},{13,9},{2,14},{6,2},{... | collective-permute-start | bytes 1572872 | tf_op jit(solution)/shard_map/ppermute | solution.py:30
  32.5 2.4 %collective-permute-start.3 = (bf16[2,256,512]{2,1,0:T(8,128)(2,1)S(1)}, bf16[2,256,512]{2,1,0:T(8,128)(2,1)}, u32[]{:S(2)}, u32[]{:S(2)}) collective-permute-start(bf16[2,256,512]{2,1,0:T(8,128)(2,1)S(1)} %pair.1.refs_0_), channel_id=1, source_target_pairs={{0,8},{4,12},{8,0},{12,4},{1,9},{5,13},{9,1},{13,5},{2,10},{6,14},... | collective-permute-start | bytes 1572872 | tf_op jit(solution)/shard_map/ppermute | solution.py:30
  34.9 2.5 %collective-permute-start.2 = (bf16[2,256,512]{2,1,0:T(8,128)(2,1)S(1)}, bf16[2,256,512]{2,1,0:T(8,128)(2,1)}, u32[]{:S(2)}, u32[]{:S(2)}) collective-permute-start(bf16[2,256,512]{2,1,0:T(8,128)(2,1)S(1)} %pair.1.refs_0_), channel_id=1, source_target_pairs={{0,4},{4,8},{8,12},{12,0},{1,5},{5,9},{9,13},{13,1},{2,6},{6,10},{... | collective-permute-start | bytes 1572872 | tf_op jit(solution)/shard_map/ppermute | solution.py:30
  37.4 12.9 %all-to-all-start.1 = ((bf16[4,32,512]{2,1,0:T(8,128)(2,1)}), bf16[4,32,512]{2,1,0:T(8,128)(2,1)S(1)}, u32[]{:S(2)}, u32[]{:S(2)}) async-start(bf16[4,32,512]{2,1,0:T(8,128)(2,1)} %near_sum.1._), calls=%async_computation.1 | async-start | bytes 262144 | tf_op jit(solution)/shard_map/all_to_all | solution.py:213
  50.3 1.6 %collective-permute-done.5.came = bf16[4,256,512]{2,1,0:T(8,128)(2,1)} collective-permute-done((bf16[4,256,512]{2,1,0:T(8,128)(2,1)}, bf16[4,256,512]{2,1,0:T(8,128)(2,1)}, u32[]{:S(2)}, u32[]{:S(2)}) %collective-permute-start.5) | collective-permute-done | bytes 1048608 | tf_op jit(solution)/shard_map/ppermute | solution.py:30
  51.9 2.7 %kept_terms.1 = (bf16[256,512]{1,0:T(8,128)(2,1)S(1)}, bf16[256,512]{1,0:T(8,128)(2,1)}, bf16[256,512]{1,0:T(8,128)(2,1)}, bf16[256,512]{1,0:T(8,128)(2,1)}) custom-call(bf16[192,4096]{1,0:T(8,128)(2,1)S(1)} %copy-done, bf16[192,512]{1,0:T(8,128)(2,1)S(1)} %copy-done.1, bf16[192,2560]{1,0:T(8,128)(2,1)S(1)} %collective-permute-done.other, ...), custom_call_target="tpu_custom_call" | custom-call | flops 1000000000 | bytes 262144 | tf_op jit(solution)/shard_map/kept_terms/pallas_call | solution.py:44
  54.6 0.0 copy-start.10
  54.6 0.7 copy-done.10
  55.3 2.2 %collective-permute-start.7 = (bf16[256,512]{1,0:T(8,128)(2,1)}, bf16[256,512]{1,0:T(8,128)(2,1)S(1)}, u32[]{:S(2)}, u32[]{:S(2)}) collective-permute-start(bf16[256,512]{1,0:T(8,128)(2,1)} %get-tuple-element.22), channel_id=1, source_target_pairs={{0,8},{4,12},{8,0},{12,4},{1,9},{5,13},{9,1},{13,5},{2,10},{6,14},... | collective-permute-start | bytes 786440 | tf_op jit(solution)/shard_map/ppermute | solution.py:30
  57.5 4.0 %collective-permute-start.9 = (bf16[256,512]{1,0:T(8,128)(2,1)}, bf16[256,512]{1,0:T(8,128)(2,1)}, u32[]{:S(2)}, u32[]{:S(2)}) collective-permute-start(bf16[256,512]{1,0:T(8,128)(2,1)} %get-tuple-element.23), channel_id=1, source_target_pairs={{0,12},{4,0},{8,4},{12,8},{1,13},{5,1},{9,5},{13,9},{2,14},{6,2},{... | collective-permute-start | bytes 786440 | tf_op jit(solution)/shard_map/ppermute | solution.py:30
  61.5 0.0 collective-permute-done.4.refs_3_
  61.5 1.9 %collective-permute-start.8 = (bf16[256,512]{1,0:T(8,128)(2,1)}, bf16[256,512]{1,0:T(8,128)(2,1)}, u32[]{:S(2)}, u32[]{:S(2)}) collective-permute-start(bf16[256,512]{1,0:T(8,128)(2,1)} %get-tuple-element.18.refs_5_.rest_0_), channel_id=1, source_target_pairs={{0,4},{4,8},{8,12},{12,0},{1,5},{5,9},{9,13},{13,1},{2,6},{6,10},{... | collective-permute-start | bytes 786440 | tf_op jit(solution)/shard_map/ppermute | solution.py:30
  63.4 0.0 all-to-all-done.1.refs_4_.parts
  63.4 0.7 far_sum.1
  64.2 3.8 %all-to-all-start.2 = ((bf16[8,32,512]{2,1,0:T(8,128)(2,1)}), bf16[8,32,512]{2,1,0:T(8,128)(2,1)S(1)}, u32[]{:S(2)}, u32[]{:S(2)}) async-start(bf16[8,32,512]{2,1,0:T(8,128)(2,1)} %far_sum.1), calls=%async_computation.2 | async-start | bytes 524288 | tf_op jit(solution)/shard_map/all_to_all | solution.py:228
  68.0 0.0 copy-start.4
  68.0 0.0 copy-start.8
  68.0 0.0 copy-start.9
  68.0 0.0 copy-start.11
  68.0 0.0 collective-permute-done.3.refs_2_
  68.1 0.0 collective-permute-done.2.refs_1_
  68.1 2.5 %input_grad_columns.1 = (bf16[192,2048]{1,0:T(8,128)(2,1)S(1)}, bf16[192,2048]{1,0:T(8,128)(2,1)S(1)}) custom-call(bf16[192,512]{1,0:T(8,128)(2,1)S(1)} %copy-done.1, bf16[192,2560]{1,0:T(8,128)(2,1)S(1)} %collective-permute-done.other, bf16[2,256,512]{2,1,0:T(8,128)(2,1)S(1)} %pair.1.refs_0_, bf16[2,256,512]{2,1,0:T(8,128)(2,1)} %collective-permute-done.2.refs_1_, ...), custom_call_target="tpu_custom_call" | custom-call | bytes 262144 | tf_op jit(solution)/shard_map/input_grad_columns/pallas_call | solution.py:44
  70.6 5.5 %collective-permute-start.6 = (bf16[192,2048]{1,0:T(8,128)(2,1)S(1)}, bf16[192,2048]{1,0:T(8,128)(2,1)S(1)}, u32[]{:S(2)}, u32[]{:S(2)}) collective-permute-start(bf16[192,2048]{1,0:T(8,128)(2,1)S(1)} %get-tuple-element.20), channel_id=1, source_target_pairs={{0,1},{1,0},{2,3},{3,2},{4,5},{5,4},{6,7},{7,6},{8,9},{9,8},{10,11... | collective-permute-start | bytes 2359304 | tf_op jit(solution)/shard_map/ppermute | solution.py:30
  76.1 0.0 collective-permute-done.7.t1
  76.1 0.0 collective-permute-done.9.t3
  76.1 0.0 collective-permute-done.8.t2
  76.1 0.0 copy-done.4
  76.1 0.0 copy-done.8
  76.1 0.0 copy-done.9
  76.1 0.0 copy-done.11
  76.2 2.1 %adam.1 = (f32[256,512]{1,0:T(8,128)S(1)}, bf16[1,256,512]{2,1,0:T(8,128)(2,1)}, bf16[1,256,512]{2,1,0:T(8,128)(2,1)}) custom-call(bf16[256,512]{1,0:T(8,128)(2,1)S(1)} %copy-done.11, bf16[256,512]{1,0:T(8,128)(2,1)S(1)} %collective-permute-done.7.t1, bf16[256,512]{1,0:T(8,128)(2,1)} %collective-permute-done.8.t2, ...), custom_call_target="tpu_custom_call" | custom-call | flops 8000000000 | bytes 262144 | tf_op jit(solution)/shard_map/adam/pallas_call | solution.py:44
  78.2 0.0 collective-permute-done.6.mate
  78.3 0.0 copy-start.7
  78.3 1.3 %input_grad.1 = bf16[192,4096]{1,0:T(8,128)(2,1)} custom-call(bf16[192,2048]{1,0:T(8,128)(2,1)S(1)} %get-tuple-element.19.own, bf16[192,2048]{1,0:T(8,128)(2,1)S(1)} %collective-permute-done.6.mate), custom_call_target="tpu_custom_call" | custom-call | bytes 262144 | tf_op jit(solution)/shard_map/input_grad/pallas_call | solution.py:44
  79.6 0.0 all-to-all-done.2
  79.6 0.0 copy-done.7
  79.6 0.8 mix.1
  (1 shorter events, 0.0 us)
Async XLA Ops:
  0.6 22.6 %copy-start.1 = (bf16[192,512]{1,0:T(8,128)(2,1)S(1)}, bf16[192,512]{1,0:T(8,128)(2,1)}, u32[]{:S(2)}) copy-start(bf16[192,512]{1,0:T(8,128)(2,1)} %cot.7) | copy-start | bytes 589828
  0.6 22.6 %copy-start = (bf16[192,4096]{1,0:T(8,128)(2,1)S(1)}, bf16[192,4096]{1,0:T(8,128)(2,1)}, u32[]{:S(2)}) copy-start(bf16[192,4096]{1,0:T(8,128)(2,1)} %acts.5) | copy-start | bytes 4718596
  0.7 11.3 %copy-start.2 = (bf16[1,256,512]{2,1,0:T(8,128)(2,1)S(1)}, bf16[1,256,512]{2,1,0:T(8,128)(2,1)}, u32[]{:S(2)}) copy-start(bf16[1,256,512]{2,1,0:T(8,128)(2,1)} %weight.3) | copy-start | bytes 786436
  0.7 13.2 %copy-start.6 = (f32[1,1,8,512]{3,2,1,0:T(8,128)S(1)}, f32[1,1,8,512]{3,2,1,0:T(8,128)}, u32[]{:S(2)}) copy-start(f32[1,1,8,512]{3,2,1,0:T(8,128)} %momentum.3) | copy-start | bytes 49156
  0.7 13.2 %copy-start.5 = (f32[1,1,8,512]{3,2,1,0:T(8,128)S(1)}, f32[1,1,8,512]{3,2,1,0:T(8,128)}, u32[]{:S(2)}) copy-start(f32[1,1,8,512]{3,2,1,0:T(8,128)} %globe.3) | copy-start | bytes 49156
  3.1 20.1 %collective-permute-start = (bf16[192,2560]{1,0:T(8,128)(2,1)}, bf16[192,2560]{1,0:T(8,128)(2,1)S(1)}, u32[]{:S(2)}, u32[]{:S(2)}) collective-permute-start(bf16[192,2560]{1,0:T(8,128)(2,1)} %pack.1), channel_id=1, source_target_pairs={{0,1},{1,0},{2,3},{3,2},{4,5},{5,4},{6,7},{7,6},{8,9},{9,8},{10,11... | collective-permute-start | bytes 2949128 | tf_op jit(solution)/shard_map/ppermute | solution.py:30
  11.9 11.3 %collective-permute-start.1 = (bf16[256,512]{1,0:T(8,128)(2,1)S(1)}, bf16[256,512]{1,0:T(8,128)(2,1)S(1)}, u32[]{:S(2)}, u32[]{:S(2)}) collective-permute-start(bf16[256,512]{1,0:T(8,128)(2,1)S(1)} %bitcast.3), channel_id=1, source_target_pairs={{0,2},{2,0},{1,3},{3,1},{4,6},{6,4},{5,7},{7,5},{8,10},{10,8},{9,1... | collective-permute-start | bytes 786440 | tf_op jit(solution)/shard_map/ppermute | solution.py:30
  14.6 12.5 %all-to-all-start = ((bf16[8,32,512]{2,1,0:T(8,128)(2,1)}), bf16[8,32,512]{2,1,0:T(8,128)(2,1)S(1)}, u32[]{:S(2)}, u32[]{:S(2)}) async-start(bf16[8,32,512]{2,1,0:T(8,128)(2,1)} %bitcast.1), calls=%async_computation | async-start | bytes 524288 | tf_op jit(solution)/shard_map/all_to_all | solution.py:199
  25.0 26.9 %collective-permute-start.5 = (bf16[4,256,512]{2,1,0:T(8,128)(2,1)}, bf16[4,256,512]{2,1,0:T(8,128)(2,1)}, u32[]{:S(2)}, u32[]{:S(2)}) collective-permute-start(bf16[4,256,512]{2,1,0:T(8,128)(2,1)} %sent_terms.1), channel_id=1, source_target_pairs={{0,2},{2,0},{1,3},{3,1},{4,6},{6,4},{5,7},{7,5},{8,10},{10,8},{9,1... | collective-permute-start | bytes 3145736 | tf_op jit(solution)/shard_map/ppermute | solution.py:30
  27.8 0.9 %copy-start.3 = (bf16[1,256,512]{2,1,0:T(8,128)(2,1)S(1)}, bf16[1,256,512]{2,1,0:T(8,128)(2,1)}, u32[]{:S(2)}) copy-start(bf16[1,256,512]{2,1,0:T(8,128)(2,1)} %weight.3) | copy-start | bytes 786436
  28.8 32.6 %collective-permute-start.4 = (bf16[2,256,512]{2,1,0:T(8,128)(2,1)S(1)}, bf16[2,256,512]{2,1,0:T(8,128)(2,1)}, u32[]{:S(2)}, u32[]{:S(2)}) collective-permute-start(bf16[2,256,512]{2,1,0:T(8,128)(2,1)S(1)} %pair.1.refs_0_), channel_id=1, source_target_pairs={{0,12},{4,0},{8,4},{12,8},{1,13},{5,1},{9,5},{13,9},{2,14},{6,2},{... | collective-permute-start | bytes 1572872 | tf_op jit(solution)/shard_map/ppermute | solution.py:30
  32.5 35.6 %collective-permute-start.3 = (bf16[2,256,512]{2,1,0:T(8,128)(2,1)S(1)}, bf16[2,256,512]{2,1,0:T(8,128)(2,1)}, u32[]{:S(2)}, u32[]{:S(2)}) collective-permute-start(bf16[2,256,512]{2,1,0:T(8,128)(2,1)S(1)} %pair.1.refs_0_), channel_id=1, source_target_pairs={{0,8},{4,12},{8,0},{12,4},{1,9},{5,13},{9,1},{13,5},{2,10},{6,14},... | collective-permute-start | bytes 1572872 | tf_op jit(solution)/shard_map/ppermute | solution.py:30
  34.9 33.2 %collective-permute-start.2 = (bf16[2,256,512]{2,1,0:T(8,128)(2,1)S(1)}, bf16[2,256,512]{2,1,0:T(8,128)(2,1)}, u32[]{:S(2)}, u32[]{:S(2)}) collective-permute-start(bf16[2,256,512]{2,1,0:T(8,128)(2,1)S(1)} %pair.1.refs_0_), channel_id=1, source_target_pairs={{0,4},{4,8},{8,12},{12,0},{1,5},{5,9},{9,13},{13,1},{2,6},{6,10},{... | collective-permute-start | bytes 1572872 | tf_op jit(solution)/shard_map/ppermute | solution.py:30
  37.4 26.0 %all-to-all-start.1 = ((bf16[4,32,512]{2,1,0:T(8,128)(2,1)}), bf16[4,32,512]{2,1,0:T(8,128)(2,1)S(1)}, u32[]{:S(2)}, u32[]{:S(2)}) async-start(bf16[4,32,512]{2,1,0:T(8,128)(2,1)} %near_sum.1._), calls=%async_computation.1 | async-start | bytes 262144 | tf_op jit(solution)/shard_map/all_to_all | solution.py:213
  54.6 0.7 copy-start.10
  55.3 20.8 %collective-permute-start.7 = (bf16[256,512]{1,0:T(8,128)(2,1)}, bf16[256,512]{1,0:T(8,128)(2,1)S(1)}, u32[]{:S(2)}, u32[]{:S(2)}) collective-permute-start(bf16[256,512]{1,0:T(8,128)(2,1)} %get-tuple-element.22), channel_id=1, source_target_pairs={{0,8},{4,12},{8,0},{12,4},{1,9},{5,13},{9,1},{13,5},{2,10},{6,14},... | collective-permute-start | bytes 786440 | tf_op jit(solution)/shard_map/ppermute | solution.py:30
  57.5 18.6 %collective-permute-start.9 = (bf16[256,512]{1,0:T(8,128)(2,1)}, bf16[256,512]{1,0:T(8,128)(2,1)}, u32[]{:S(2)}, u32[]{:S(2)}) collective-permute-start(bf16[256,512]{1,0:T(8,128)(2,1)} %get-tuple-element.23), channel_id=1, source_target_pairs={{0,12},{4,0},{8,4},{12,8},{1,13},{5,1},{9,5},{13,9},{2,14},{6,2},{... | collective-permute-start | bytes 786440 | tf_op jit(solution)/shard_map/ppermute | solution.py:30
  61.5 14.6 %collective-permute-start.8 = (bf16[256,512]{1,0:T(8,128)(2,1)}, bf16[256,512]{1,0:T(8,128)(2,1)}, u32[]{:S(2)}, u32[]{:S(2)}) collective-permute-start(bf16[256,512]{1,0:T(8,128)(2,1)} %get-tuple-element.18.refs_5_.rest_0_), channel_id=1, source_target_pairs={{0,4},{4,8},{8,12},{12,0},{1,5},{5,9},{9,13},{13,1},{2,6},{6,10},{... | collective-permute-start | bytes 786440 | tf_op jit(solution)/shard_map/ppermute | solution.py:30
  64.2 15.4 %all-to-all-start.2 = ((bf16[8,32,512]{2,1,0:T(8,128)(2,1)}), bf16[8,32,512]{2,1,0:T(8,128)(2,1)S(1)}, u32[]{:S(2)}, u32[]{:S(2)}) async-start(bf16[8,32,512]{2,1,0:T(8,128)(2,1)} %far_sum.1), calls=%async_computation.2 | async-start | bytes 524288 | tf_op jit(solution)/shard_map/all_to_all | solution.py:228
  68.0 8.1 %copy-start.4 = (bf16[1,256,512]{2,1,0:T(8,128)(2,1)S(1)}, bf16[1,256,512]{2,1,0:T(8,128)(2,1)}, u32[]{:S(2)}) copy-start(bf16[1,256,512]{2,1,0:T(8,128)(2,1)} %weight.3) | copy-start | bytes 786436
  68.0 8.1 %copy-start.8 = (bf16[1,256,512]{2,1,0:T(8,128)(2,1)S(1)}, bf16[1,256,512]{2,1,0:T(8,128)(2,1)}, u32[]{:S(2)}) copy-start(bf16[1,256,512]{2,1,0:T(8,128)(2,1)} %adam_first.1) | copy-start | bytes 786436
  68.0 8.1 %copy-start.9 = (bf16[1,256,512]{2,1,0:T(8,128)(2,1)S(1)}, bf16[1,256,512]{2,1,0:T(8,128)(2,1)}, u32[]{:S(2)}) copy-start(bf16[1,256,512]{2,1,0:T(8,128)(2,1)} %adam_second.1) | copy-start | bytes 786436
  68.0 8.1 %copy-start.11 = (bf16[256,512]{1,0:T(8,128)(2,1)S(1)}, bf16[256,512]{1,0:T(8,128)(2,1)}, u32[]{:S(2)}) copy-start(bf16[256,512]{1,0:T(8,128)(2,1)} %copy-done.10) | copy-start | bytes 786436
  70.6 7.7 %collective-permute-start.6 = (bf16[192,2048]{1,0:T(8,128)(2,1)S(1)}, bf16[192,2048]{1,0:T(8,128)(2,1)S(1)}, u32[]{:S(2)}, u32[]{:S(2)}) collective-permute-start(bf16[192,2048]{1,0:T(8,128)(2,1)S(1)} %get-tuple-element.20), channel_id=1, source_target_pairs={{0,1},{1,0},{2,3},{3,2},{4,5},{5,4},{6,7},{7,6},{8,9},{9,8},{10,11... | collective-permute-start | bytes 2359304 | tf_op jit(solution)/shard_map/ppermute | solution.py:30
  78.3 1.4 %copy-start.7 = (f32[1,1,8,512]{3,2,1,0:T(8,128)S(1)}, f32[1,1,8,512]{3,2,1,0:T(8,128)}, u32[]{:S(2)}) copy-start(f32[1,1,8,512]{3,2,1,0:T(8,128)} %momentum.3) | copy-start | bytes 49156
